TPU v7x, 512 devices: a whole 4x8x8 slice. The times are simulated.
512 devices in a mesh: shard: 32 (over y_hi, z), layer: 16 (over x, y_lo, core).
Axes of the slice: x: 4, y: 8 (y_hi: 4, y_lo: 2; y = y_hi * 2 + y_lo), z: 8, core: 2. Of those that a mesh axis runs over, the one named last changes fastest.
Arguments:
- query_grads: bfloat16 [128, 48, 4096], P('shard', 'layer'), may hold values from -12 to 12
- out_basis: float32 [48, 64, 64], P('layer'), may hold values from -0.2 to 1.2
- in_basis: float32 [48, 64, 64], P('layer'), may hold values from -0.2 to 1.2
- eigen_scale: float32 [48, 64, 64], P('layer'), may hold values from 0.05 to 5
- layer_slot: int32 [48], P('layer'), may hold values from 0 to 47, as said below
- train_grads: bfloat16 [1024, 48, 4096], P('shard', 'layer'), may hold values from -6 to 6
Outputs:
- scores: float32 [128, 1024], P('layer', 'shard')
Inputs may be any that keep to these rules, and one draw needn't show every extreme that they name: `layer_slot`: slot s holds one of the layers s - s % 3 to s - s % 3 + 2, and each layer is held by exactly one slot.
All inputs are finite; a program needn't handle non-finite values.
Results may differ from a plain program's by a relative error of at most 0.0029.
Values may be sent and summed in bfloat16 or wider, within the bound.
A program may use at most 64 MiB of HBM per device.

v0:
```python
import jax
import jax.numpy as jnp
from jax import lax
from jax.sharding import PartitionSpec as P

DAMPING = 0.05
EPSILON = 1e-06


def precondition_layer(blocks, left_basis, right_basis, eigen_values):
    high = lax.Precision.HIGHEST
    rotated = jnp.einsum("ab,nac->nbc", left_basis, blocks, precision=high)
    rotated = jnp.einsum("nbc,cd->nbd", rotated, right_basis, precision=high)
    rotated = rotated / (eigen_values + DAMPING)
    back = jnp.einsum("ab,nbd->nad", left_basis, rotated, precision=high)
    return jnp.einsum("nad,cd->nac", back, right_basis, precision=high)


def precondition_all(queries, out_basis, in_basis, eigen_scale):
    count = queries.shape[0]
    depth = queries.shape[1]
    width = queries.shape[2]
    side = out_basis.shape[1]
    pieces = []
    for layer_index in range(depth):
        blocks = queries[:, layer_index].astype(jnp.float32).reshape(count, side, side)
        result = precondition_layer(
            blocks, out_basis[layer_index], in_basis[layer_index], eigen_scale[layer_index]
        )
        pieces.append(result.reshape(count, width).astype(jnp.bfloat16))
    return jnp.stack(pieces, axis=1)


def on_device(query_grads, out_basis, in_basis, eigen_scale, layer_slot, train_grads):
    gathered = lax.all_gather(query_grads, "shard", axis=0, tiled=True)
    precond = precondition_all(gathered, out_basis, in_basis, eigen_scale)
    count = precond.shape[0]
    depth = precond.shape[1]
    width = precond.shape[2]
    group = lax.axis_index("layer")
    local_slot = layer_slot - group * depth
    selector = (local_slot[:, None] == jnp.arange(depth, dtype=jnp.int32)[None, :]).astype(
        jnp.bfloat16
    )
    ordered = jnp.einsum(
        "sl,nlf->nsf", selector, precond, preferred_element_type=jnp.float32
    ).astype(jnp.bfloat16)
    rows = train_grads.shape[0]
    partial_scores = lax.dot_general(
        ordered.reshape(count, depth * width),
        train_grads.reshape(rows, depth * width),
        (((1,), (1,)), ((), ())),
        preferred_element_type=jnp.float32,
    )
    wide = precond.astype(jnp.float32)
    partial_norm = jnp.sum(wide * wide, axis=(1, 2))
    mine = count // lax.axis_size("layer")
    norm_total = lax.psum(partial_norm, "layer")
    norm_mine = lax.dynamic_slice_in_dim(norm_total, group * mine, mine, 0)
    summed = lax.psum_scatter(partial_scores, "layer", scatter_dimension=0, tiled=True)
    return summed / jnp.sqrt(norm_mine + EPSILON)[:, None]


def solution(mesh):
    return jax.shard_map(
        on_device,
        mesh=mesh,
        in_specs=(
            P("shard", "layer", None),
            P("layer", None, None),
            P("layer", None, None),
            P("layer", None, None),
            P("layer"),
            P("shard", "layer", None),
        ),
        out_specs=P("layer", "shard"),
        check_vma=False,
    )
```

profile of v0, /device:TPU:1, one launch (start us, length us, event | category | flops | bytes accessed | tf_op | source)
XLA Modules:
  0.0 325.4 jit_solution(7543624098246859757)
XLA Ops:
  6.5 0.0 copy-start
  6.5 0.0 all-gather.2.cloned.1.call-start
  6.5 1.7 copy.8
  8.2 0.0 all-gather.2.cloned.1.call-update
  8.3 1.3 dynamic-slice
  10.2 0.7 broadcast_subtract_fusion
  10.8 0.8 add_bitcast_fusion.2
  11.6 105.0 %all-gather.2.cloned.1.call-done = bf16[128,3,4096]{2,1,0:T(4,128)(2,1)} async-done(((bf16[4,3,4096]{2,1,0:T(4,128)(2,1)}), bf16[128,3,4096]{2,1,0:T(4,128)(2,1)}) %all-gather.2.cloned.1.call-update) | async-done | bytes 3145744 | tf_op jit(solution)/shard_map/all_gather | solution.py:35
  116.7 12.2 %fusion.60 = (bf16[128,1,4096]{2,1,0:T(2,128)(2,1)S(1)}, bf16[128,1,4096]{2,1,0:T(2,128)(2,1)}, bf16[128,1,4096]{2,1,0:T(2,128)(2,1)}) fusion(bf16[128,3,4096]{2,1,0:T(4,128)(2,1)} %all-gather.2.cloned.1.call-done), kind=kLoop, calls=%fused_computation.64 | loop fusion | bytes 6291456 | tf_op jit(solution)/shard_map/slice | solution.py:26
  128.8 0.0 copy-start.5
  128.8 3.6 %copy.34 = bf16[128,1,4096]{0,2,1:T(8,128)(2,1)} copy(bf16[128,1,4096]{2,1,0:T(2,128)(2,1)S(1)} %get-tuple-element.9) | data formatting | bytes 2097152
  132.4 0.0 copy-start.4
  132.4 5.0 %copy.10 = bf16[128,64,64]{1,2,0:T(8,128)(2,1)S(1)} copy(bf16[128,64,64]{0,2,1:T(8,128)(2,1)} %bitcast.79) | data formatting | bytes 2097152 | tf_op jit(solution)/shard_map/reshape | solution.py:26
  137.3 0.0 copy-done.5
  137.4 1.8 fusion.43
  139.2 0.0 copy-done.4
  139.2 6.7 %fusion.5 = f32[128,64,64]{2,1,0:T(8,128)S(1)} fusion(f32[128,64,64]{2,1,0:T(8,128)S(1)} %fusion.43, f32[3,64,64]{2,1,0:T(8,128)S(1)} %copy-done.4), kind=kOutput, calls=%fused_computation.8 | convolution fusion | flops 402653184 | bytes 6324224 | tf_op jit(solution)/shard_map/nbc,cd->nbd/dot_general | solution.py:13
  145.9 8.5 %fusion.15 = f32[128,64,64]{1,2,0:T(8,128)} fusion(f32[128,64,64]{2,1,0:T(8,128)S(1)} %fusion.5, f32[64,64]{1,0:T(8,128)S(1)} %get-tuple-element.12, f32[3,64,64]{2,1,0:T(8,128)S(1)} %copy-done.5), kind=kOutput, calls=%fused_computation.18 | convolution fusion | flops 403177472 | bytes 6356992 | tf_op jit(solution)/shard_map/ab,nbd->nad/dot_general | solution.py:15
  154.4 4.5 %copy.13 = f32[128,64,64]{0,2,1:T(8,128)S(1)} copy(f32[128,64,64]{1,2,0:T(8,128)} %fusion.15) | data formatting | bytes 4194304 | tf_op jit(solution)/shard_map/ab,nbd->nad/transpose | solution.py:15
  158.9 3.0 convolution_convert_fusion.3
  161.9 0.0 copy-start.3
  161.9 5.7 %copy.24 = bf16[128,1,4096]{2,1,0:T(2,128)(2,1)} copy(bf16[128,1,4096]{0,2,1:T(8,128)(2,1)} %bitcast.80) | data formatting | bytes 2097152 | tf_op jit(solution)/shard_map/convert_element_type | solution.py:30
  167.5 0.0 copy-done.3
  167.5 3.6 %copy.35 = bf16[128,1,4096]{0,2,1:T(8,128)(2,1)} copy(bf16[128,1,4096]{2,1,0:T(2,128)(2,1)S(1)} %copy-done.3) | data formatting | bytes 2097152
  171.1 5.2 %copy.15 = bf16[128,64,64]{1,2,0:T(8,128)(2,1)S(1)} copy(bf16[128,64,64]{0,2,1:T(8,128)(2,1)} %bitcast.81) | data formatting | bytes 2097152 | tf_op jit(solution)/shard_map/reshape | solution.py:26
  176.3 1.8 fusion.38
  178.1 6.7 %fusion.3 = f32[128,64,64]{2,1,0:T(8,128)S(1)} fusion(f32[128,64,64]{2,1,0:T(8,128)S(1)} %fusion.38, f32[3,64,64]{2,1,0:T(8,128)S(1)} %copy-done.4), kind=kOutput, calls=%fused_computation.6 | convolution fusion | flops 402653184 | bytes 6324224 | tf_op jit(solution)/shard_map/nbc,cd->nbd/dot_general | solution.py:13
  184.8 8.4 %fusion.18 = f32[128,64,64]{1,2,0:T(8,128)} fusion(f32[128,64,64]{2,1,0:T(8,128)S(1)} %fusion.3, f32[64,64]{1,0:T(8,128)S(1)} %get-tuple-element.14, f32[3,64,64]{2,1,0:T(8,128)S(1)} %copy-done.5), kind=kOutput, calls=%fused_computation.19 | convolution fusion | flops 403177472 | bytes 6356992 | tf_op jit(solution)/shard_map/ab,nbd->nad/dot_general | solution.py:15
  193.2 4.5 %copy.18 = f32[128,64,64]{0,2,1:T(8,128)S(1)} copy(f32[128,64,64]{1,2,0:T(8,128)} %fusion.18) | data formatting | bytes 4194304 | tf_op jit(solution)/shard_map/ab,nbd->nad/transpose | solution.py:15
  197.7 3.0 convolution_convert_fusion.2
  200.7 5.7 %copy.25 = bf16[128,1,4096]{2,1,0:T(2,128)(2,1)} copy(bf16[128,1,4096]{0,2,1:T(8,128)(2,1)} %bitcast.82) | data formatting | bytes 2097152 | tf_op jit(solution)/shard_map/convert_element_type | solution.py:30
  206.4 0.0 copy-done.2
  206.4 3.6 %copy.36 = bf16[128,1,4096]{0,2,1:T(8,128)(2,1)} copy(bf16[128,1,4096]{2,1,0:T(2,128)(2,1)S(1)} %copy-done.2) | data formatting | bytes 2097152
  209.9 4.9 %copy.20 = bf16[128,64,64]{1,2,0:T(8,128)(2,1)S(1)} copy(bf16[128,64,64]{0,2,1:T(8,128)(2,1)} %bitcast.83) | data formatting | bytes 2097152 | tf_op jit(solution)/shard_map/reshape | solution.py:26
  214.9 1.8 fusion.33
  216.7 6.7 %fusion.1 = f32[128,64,64]{2,1,0:T(8,128)S(1)} fusion(f32[128,64,64]{2,1,0:T(8,128)S(1)} %fusion.33, f32[3,64,64]{2,1,0:T(8,128)S(1)} %copy-done.4), kind=kOutput, calls=%fused_computation.4 | convolution fusion | flops 402653184 | bytes 6324224 | tf_op jit(solution)/shard_map/nbc,cd->nbd/dot_general | solution.py:13
  223.4 8.5 %fusion.21 = f32[128,64,64]{1,2,0:T(8,128)} fusion(f32[128,64,64]{2,1,0:T(8,128)S(1)} %fusion.1, f32[64,64]{1,0:T(8,128)S(1)} %get-tuple-element.13, f32[3,64,64]{2,1,0:T(8,128)S(1)} %copy-done.5), kind=kOutput, calls=%fused_computation.20 | convolution fusion | flops 403177472 | bytes 6356992 | tf_op jit(solution)/shard_map/ab,nbd->nad/dot_general | solution.py:15
  231.8 4.5 %copy.23 = f32[128,64,64]{0,2,1:T(8,128)S(1)} copy(f32[128,64,64]{1,2,0:T(8,128)} %fusion.21) | data formatting | bytes 4194304 | tf_op jit(solution)/shard_map/ab,nbd->nad/transpose | solution.py:15
  236.4 3.0 convolution_convert_fusion.1
  239.3 5.6 %copy.26 = bf16[128,1,4096]{2,1,0:T(2,128)(2,1)} copy(bf16[128,1,4096]{0,2,1:T(8,128)(2,1)} %bitcast.84) | data formatting | bytes 2097152 | tf_op jit(solution)/shard_map/convert_element_type | solution.py:30
  245.0 0.0 copy-done.1
  245.0 12.6 %multiply_reduce_fusion = (f32[128]{0:T(128)S(1)}, bf16[128,3,4096]{2,1,0:T(4,128)(2,1)S(1)}) fusion(bf16[128,1,4096]{2,1,0:T(2,128)(2,1)} %copy.26, bf16[128,1,4096]{2,1,0:T(2,128)(2,1)} %copy.25, bf16[128,1,4096]{2,1,0:T(2,128)(2,1)S(1)} %copy-done.1), kind=kLoop, calls=%fused_computation | loop fusion | flops 14155648 | bytes 6291968 | tf_op jit(solution)/shard_map/reduce_sum | solution.py:56
  257.6 2.5 fusion
  260.1 0.0 copy-done
  260.1 3.4 %fusion.27 = f32[128,32]{1,0:T(8,128)S(1)} fusion(bf16[32,3,4096]{2,0,1:T(8,128)(2,1)S(1)} %copy-done, bf16[128,3,4096]{2,1,0:T(4,128)(2,1)S(1)} %fusion), kind=kOutput, calls=%fused_computation.27 | convolution fusion | flops 100663296 | bytes 3948544 | tf_op jit(solution)/shard_map/dot_general | solution.py:49
  263.6 53.8 %all-reduce.1 = (f32[128,32]{1,0:T(8,128)S(1)}, f32[128]{0:T(128)S(1)}) all-reduce(f32[128,32]{1,0:T(8,128)S(1)} %fusion.27, f32[128]{0:T(128)S(1)} %get-tuple-element.7), channel_id=2, replica_groups=mesh['shard'=32,'layer'=16] {'layer'}, use_global_device_ids=true, to_apply=%region_0.0.clone | all-reduce | flops 4224 | bytes 33792
  317.3 0.1 add_sqrt_fusion
  317.4 0.7 dynamic-slice_divide_fusion
  (2 shorter events, 0.0 us)
Async XLA Ops:
  6.5 253.6 %copy-start = (bf16[32,3,4096]{2,0,1:T(8,128)(2,1)S(1)}, bf16[32,3,4096]{2,0,1:T(8,128)(2,1)}, u32[]{:S(2)}) copy-start(bf16[32,3,4096]{2,0,1:T(8,128)(2,1)} %param.11) | copy-start | bytes 2359300
  6.5 110.1 %all-gather.2.cloned.1.call-start = ((), (), s32[]{:S(2)}) async-start(), calls=%async_computation | async-start | bytes 4325376 | tf_op jit(solution)/shard_map/all_gather | solution.py:35
  128.8 8.5 %copy-start.5 = (f32[3,64,64]{2,1,0:T(8,128)S(1)}, f32[3,64,64]{2,1,0:T(8,128)}, u32[]{:S(2)}) copy-start(f32[3,64,64]{2,1,0:T(8,128)} %param.7) | copy-start | bytes 147460
  132.4 6.8 %copy-start.4 = (f32[3,64,64]{2,1,0:T(8,128)S(1)}, f32[3,64,64]{2,1,0:T(8,128)}, u32[]{:S(2)}) copy-start(f32[3,64,64]{2,1,0:T(8,128)} %param.8) | copy-start | bytes 147460
  161.9 5.7 %copy-start.3 = (bf16[128,1,4096]{2,1,0:T(2,128)(2,1)S(1)}, bf16[128,1,4096]{2,1,0:T(2,128)(2,1)}, u32[]{:S(2)}) copy-start(bf16[128,1,4096]{2,1,0:T(2,128)(2,1)} %get-tuple-element.10) | copy-start | bytes 3145732
  200.7 5.7 %copy-start.2 = (bf16[128,1,4096]{2,1,0:T(2,128)(2,1)S(1)}, bf16[128,1,4096]{2,1,0:T(2,128)(2,1)}, u32[]{:S(2)}) copy-start(bf16[128,1,4096]{2,1,0:T(2,128)(2,1)} %get-tuple-element.11) | copy-start | bytes 3145732
  239.3 5.6 %copy-start.1 = (bf16[128,1,4096]{2,1,0:T(2,128)(2,1)S(1)}, bf16[128,1,4096]{2,1,0:T(2,128)(2,1)}, u32[]{:S(2)}) copy-start(bf16[128,1,4096]{2,1,0:T(2,128)(2,1)} %copy.24) | copy-start | bytes 3145732
Sparse Core Ops, SparseCore 0:
  10.5 106.0 all-gather.1
where the time goes:
time: 332 us; the launch traced here: 325 us
  waiting for transfers between devices  105 us (32%)
  local copies, waits for them, and re-layouts  71.3 us (21%)
  matrix products  65.7 us (20%)
  blocking collectives  53.8 us (16%)
  other arithmetic  14.8 us (4%)
  between operations  14.7 us (4%)
    all_gather x1, waiting for transfers between devices, on_device(): gathered = lax.all_gather(query_grads, 'shard', axis=0, tiled=True)  105 us
    unnamed x1, blocking collectives  53.8 us
    dot_general x3, matrix products, precondition_layer(): back = jnp.einsum('ab,nbd->nad', left_basis, rotated, precision=high)  25.3 us
    dot_general x3, matrix products, precondition_layer(): rotated = jnp.einsum('nbc,cd->nbd', rotated, right_basis, precision=high)  20 us
    convert_element_type x3, local copies, waits for them, and re-layouts, precondition_all(): pieces.append(result.reshape(count, width).astype(jnp.bfloat16))  16.9 us
    reshape x3, local copies, waits for them, and re-layouts, precondition_all(): queries[:, layer_index].astype(jnp.float32).reshape(count, side, side)  15.1 us
    unnamed x17, local copies, waits for them, and re-layouts  13.6 us
    transpose x3, local copies, waits for them, and re-layouts, precondition_layer(): back = jnp.einsum('ab,nbd->nad', left_basis, rotated, precision=high)  13.5 us
  transfers between devices with their start and end apart: 1, of which 1 were waited for; matrix products, arithmetic and copies ran while one was open for 1% of the time, Pallas kernels for 0%

commit v1 on v0

v1 whole, which is shorter than its diff:
```python
import functools

import jax
import jax.numpy as jnp
from jax import lax
from jax.experimental import pallas as pl
from jax.experimental.pallas import tpu as pltpu
from jax.sharding import PartitionSpec as P

DAMPING = 0.05
EPSILON = 1e-06
MESH = pl.DeviceIdType.MESH
COLUMNS = 4
OWN, FIRST, SECOND, ACROSS = range(4)


def precondition_slot(index, slot, q_ref, s_ref, a_ref, e_ref, rows_ref, turned_ref, blocks_ref):
    high = lax.Precision.HIGHEST
    side = s_ref.shape[1]
    width = q_ref.shape[2]
    pieces = width // 128
    quarter = pieces // 8
    queries = q_ref[index].astype(jnp.float32)
    for piece in range(pieces):
        rows_ref[slot, 4 * piece : 4 * piece + 4, :] = queries[:, 128 * piece : 128 * (piece + 1)]
    count = side // 4
    basis = jnp.concatenate(
        [s_ref[index, pl.ds(2 * parity + half, count, stride=4), :] for half in range(2) for parity in range(2)], axis=0
    )
    right = a_ref[index]
    scale = e_ref[index] + DAMPING
    stacked = []
    for n in range(4):
        halves = [rows_ref[slot, pl.ds(4 * parity + n, count, stride=8), :] for parity in range(2)]
        both = jnp.concatenate(halves, axis=0)
        stacked.append(jnp.concatenate([both[:, :side], both[:, side:]], axis=0))
    stacked = jnp.concatenate(stacked, axis=0)
    stacked = lax.dot_general(stacked, right, (((1,), (0,)), ((), ())), precision=high, preferred_element_type=jnp.float32)
    wide = jnp.concatenate([stacked[side * n : side * (n + 1)] for n in range(4)], axis=1)
    wide = lax.dot_general(basis.T, wide, (((1,), (0,)), ((), ())), precision=high, preferred_element_type=jnp.float32)
    wide = wide / jnp.concatenate([scale] * 4, axis=1)
    wide = lax.dot_general(basis, wide, (((1,), (0,)), ((), ())), precision=high, preferred_element_type=jnp.float32)
    stacked = jnp.concatenate([wide[:, side * n : side * (n + 1)] for n in range(4)], axis=0)
    stacked = lax.dot_general(stacked, right, (((1,), (1,)), ((), ())), precision=high, preferred_element_type=jnp.float32)
    for n in range(4):
        block = stacked[side * n : side * (n + 1)]
        lanes = jnp.concatenate([block[: side // 2], block[side // 2 :]], axis=1)
        for parity in range(2):
            turned_ref[slot, parity, pl.ds(n, count, stride=4), :] = lanes[count * parity : count * (parity + 1)]
    for parity in range(2):
        for part in range(4):
            blocks_ref[part, :, 256 * slot + 128 * parity : 256 * slot + 128 * (parity + 1)] = turned_ref[
                slot, parity, 16 * part : 16 * (part + 1), :
            ].astype(jnp.bfloat16)


def kernel(
    ring,
    groups,
    slot_ref,
    q_ref,
    s_ref,
    a_ref,
    e_ref,
    train_ref,
    out_ref,
    rows_ref,
    turned_ref,
    blocks_ref,
    train_part,
    gathered,
    total,
    squares,
    tiles,
    tiles_in,
    summed,
    summed_in,
    local_sem,
    t_send,
    t_recv,
    y_send,
    y_recv,
    z_send,
    z_recv,
    r_send,
    r_recv,
    p_send,
    p_recv,
):
    shard = lax.axis_index("shard")
    group = lax.axis_index("layer")
    column = shard // ring
    level = lax.rem(shard, ring)
    slots = q_ref.shape[0]
    reach = ring // 2
    tile_count = tiles.shape[0]

    def at(col, lev):
        return col * ring + lev

    first = column + 1 - 2 * lax.rem(column, 2)
    second = 3 - column
    across = 3 - first
    columns = [column, first, second, across]
    high_first = jnp.where((column == 1) | (column == 2), 1, 0)
    high_second = jnp.where(column >= 2, 1, 0)
    mine = [high_first, 2 + high_second]
    other = [1 - high_first, 3 - high_second]

    def remote(src, dst, send, recv, to_shard, to_group):
        return pltpu.make_async_remote_copy(
            src_ref=src, dst_ref=dst, send_sem=send, recv_sem=recv, device_id=(to_shard, to_group), device_id_type=MESH
        )

    up = at(column, lax.rem(level + 1, ring))
    down = at(column, lax.rem(level + ring - 1, ring))
    barrier = pltpu.get_barrier_semaphore()
    partners = [(up, group), (down, group)] + [(at(c, level), group) for c in columns[1:]]
    partners += [(shard, lax.rem(group + d, groups)) for d in range(1, groups)]
    for who in partners:
        pl.semaphore_signal(barrier, inc=1, device_id=who, device_id_type=MESH)
    pl.semaphore_wait(barrier, len(partners))

    span = train_ref.shape[2] // 4

    def quarter_of_train(quarter):
        return train_ref.at[:, :, pl.ds(pl.multiple_of(quarter * span, 128), span)]

    train_copies = []
    for pair in range(2):
        copy = remote(
            quarter_of_train(other[pair]),
            train_part.at[pair, 1],
            t_send.at[pair],
            t_recv.at[pair],
            at(columns[1 + pair], level),
            group,
        )
        copy.start()
        train_copies.append(copy)
    keep = []
    for pair in range(2):
        copy = pltpu.make_async_copy(quarter_of_train(mine[pair]), train_part.at[pair, 0], local_sem.at[pair])
        copy.start()
        keep.append(copy)

    for slot in range(slots):
        index = lax.rem(slot_ref[slot], slots)
        precondition_slot(index, slot, q_ref, s_ref, a_ref, e_ref, rows_ref, turned_ref, blocks_ref)

    wanted = {FIRST: [other[0], mine[1]], SECOND: [mine[0], other[1]], ACROSS: other}
    column_copies = {}
    for who in (FIRST, SECOND, ACROSS):
        for pair in range(2):
            copy = remote(
                blocks_ref.at[wanted[who][pair]],
                gathered.at[pair, column, level],
                y_send.at[who - 1, pair],
                y_recv.at[who - 1, pair],
                at(columns[who], level),
                group,
            )
            copy.start()
            column_copies[who, pair] = copy
    for pair in range(2):
        gathered[pair, column, level] = blocks_ref[mine[pair]]

    ring_copies = {}

    def runs(way, hop, who):
        return hop < reach or (who // 2 == way)

    def origin(way, hop):
        return lax.rem(level - hop + ring, ring) if way == 0 else lax.rem(level + hop, ring)

    def pass_on(way, hop, who):
        block = gathered.at[:, columns[who], origin(way, hop - 1)]
        copy = remote(
            block, block, z_send.at[way, hop - 1, who], z_recv.at[way, hop - 1, who], up if way == 0 else down, group
        )
        copy.start()
        ring_copies[way, hop, who] = copy

    def arrive(way, hop, who):
        block = gathered.at[:, columns[who], origin(way, hop)]
        remote(
            block, block, z_send.at[way, hop - 1, who], z_recv.at[way, hop - 1, who], up if way == 0 else down, group
        ).wait_recv()

    for who in (OWN, FIRST, SECOND, ACROSS):
        if who != OWN:
            for pair in range(2):
                remote(
                    blocks_ref.at[0],
                    gathered.at[pair, columns[who], level],
                    y_send.at[who - 1, pair],
                    y_recv.at[who - 1, pair],
                    at(columns[who], level),
                    group,
                ).wait_recv()
        for way in range(2):
            if runs(way, 1, who):
                pass_on(way, 1, who)

    def multiply(levels):
        for pair in range(2):
            left = [gathered[pair, :, pl.ds(lev, 1)].reshape(16 * COLUMNS, 256 * slots) for lev in levels]
            left = jnp.concatenate(left, axis=0) if len(left) > 1 else left[0]
            product = None
            for slot in range(slots):
                right = jnp.concatenate(
                    [
                        train_part[pair, who, slot, :, 256 * sub : 256 * (sub + 1)]
                        for who in range(2)
                        for sub in range(4)
                    ],
                    axis=0,
                )
                term = lax.dot_general(
                    left[:, 256 * slot : 256 * (slot + 1)],
                    right,
                    (((1,), (1,)), ((), ())),
                    preferred_element_type=jnp.float32,
                )
                product = term if product is None else product + term
            wide = left.astype(jnp.float32)
            wide = wide * wide
            norm = wide[:, :128]
            for piece in range(1, 2 * slots):
                norm = norm + wide[:, 128 * piece : 128 * (piece + 1)]
            row = lax.broadcasted_iota(jnp.int32, (16, product.shape[1]), 0) // 4
            lane = lax.rem(lax.broadcasted_iota(jnp.int32, (16, product.shape[1]), 1), 128) // 32
            same = row == lane
            for at_level, lev in enumerate(levels):
                for col in range(COLUMNS):
                    start = 16 * (COLUMNS * at_level + col)
                    kept = jnp.where(same, product[start : start + 16], 0.0)
                    total[pair, col, lev] = kept[:8] + kept[8:]
                    squares[pair, col, lev] = norm[start : start + 8] + norm[start + 8 : start + 16]

    for hop in range(1, reach + 1):
        for who in range(4):
            for way in range(2):
                if runs(way, hop, who):
                    arrive(way, hop, who)
                    if hop < reach and runs(way, hop + 1, who):
                        pass_on(way, hop + 1, who)
        if hop == 1:
            for copy in keep:
                copy.wait()
            for copy in train_copies:
                copy.wait_recv()
            multiply([level])
        if hop < reach:
            multiply([origin(0, hop), origin(1, hop)])
        else:
            multiply([origin(0, hop)])

    row = lax.broadcasted_iota(jnp.int32, (8, 128), 0)
    lane = lax.broadcasted_iota(jnp.int32, (8, 128), 1)

    def fold(value):
        value = value + pltpu.roll(value, 64, 1)
        return value + pltpu.roll(value, 32, 1)

    per_column = ring // 2
    for tile in range(tile_count):
        col, pair_of_levels = tile // per_column, tile % per_column

        def rows_of(ref, pair, lanes):
            even, odd = (ref[pair, col, 2 * pair_of_levels + k, :, lanes] for k in range(2))
            even = even + pltpu.roll(even, 4, 0)
            odd = odd + pltpu.roll(odd, 4, 0)
            return jnp.where(row < 4, even, odd)

        own = fold(rows_of(total, 0, slice(0, 128)) + rows_of(total, 1, slice(0, 128)))
        one = fold(rows_of(total, 0, slice(128, 256)))
        two = fold(rows_of(total, 1, slice(128, 256)))
        norm_one = jnp.sum(rows_of(squares, 0, slice(0, 128)), axis=1, keepdims=True)
        norm_two = jnp.sum(rows_of(squares, 1, slice(0, 128)), axis=1, keepdims=True)
        value = jnp.where(lane < 32, own, jnp.where(lane < 64, one, jnp.where(lane < 96, two, jnp.where(lane < 112, norm_one, norm_two))))
        tiles[tile] = value

    per_group = tile_count // groups
    group_copies = []
    for d in range(1, groups):
        to = lax.rem(group + d, groups)
        copy = remote(tiles.at[pl.ds(to * per_group, per_group)], tiles_in.at[d], r_send.at[d], r_recv.at[d], shard, to)
        copy.start()
        group_copies.append(copy)
    answer = tiles[pl.ds(group * per_group, per_group)]
    for copy in group_copies:
        copy.wait_recv()
    for d in range(1, groups):
        answer = answer + tiles_in[d]
    summed[...] = answer
    pair_copies = []
    for pair in range(2):
        copy = remote(summed, summed_in.at[pair], p_send.at[pair], p_recv.at[pair], at(columns[1 + pair], level), group)
        copy.start()
        pair_copies.append(copy)
    for copy in pair_copies:
        copy.wait_recv()
    from_first = summed_in[0]
    from_second = summed_in[1]
    norm = answer[:, :, 96:97] + answer[:, :, 112:113] + from_first[:, :, 96:97] + from_second[:, :, 112:113]
    raw = answer[:, :, 0:32] + from_first[:, :, 32:64] + from_second[:, :, 64:96]
    out_ref[...] = (raw / jnp.sqrt(norm + EPSILON)).reshape(out_ref.shape)

    for copy in train_copies + list(column_copies.values()) + list(ring_copies.values()) + group_copies + pair_copies:
        copy.wait_send()


def solution(mesh):
    shards, groups = mesh.shape["shard"], mesh.shape["layer"]
    ring = shards // COLUMNS

    def on_device(query_grads, out_basis, in_basis, eigen_scale, layer_slot, train_grads):
        local, slots, width = query_grads.shape
        rows = train_grads.shape[0]
        tile_count = local * shards // 8
        per_group = tile_count // groups
        reach = ring // 2
        vmem = pl.BlockSpec(memory_space=pltpu.VMEM)
        dma = pltpu.SemaphoreType.DMA
        return pl.pallas_call(
            functools.partial(kernel, ring, groups),
            out_shape=jax.ShapeDtypeStruct((8 * per_group, rows), jnp.float32),
            in_specs=[pl.BlockSpec(memory_space=pltpu.SMEM), vmem, vmem, vmem, vmem, pl.BlockSpec(memory_space=pl.ANY)],
            out_specs=vmem,
            scratch_shapes=[
                pltpu.VMEM((slots, local * width // 128, 128), jnp.float32),
                pltpu.VMEM((slots, 2, local * width // 256, 128), jnp.float32),
                pltpu.VMEM((4, 16, 256 * slots), jnp.bfloat16),
                pltpu.VMEM((2, 2, slots, rows, width // 4), jnp.bfloat16),
                pltpu.VMEM((2, COLUMNS, ring, 16, 256 * slots), jnp.bfloat16),
                pltpu.VMEM((2, COLUMNS, ring, 8, 256), jnp.float32),
                pltpu.VMEM((2, COLUMNS, ring, 8, 128), jnp.float32),
                pltpu.VMEM((tile_count, 8, 128), jnp.float32),
                pltpu.VMEM((groups, per_group, 8, 128), jnp.float32),
                pltpu.VMEM((per_group, 8, 128), jnp.float32),
                pltpu.VMEM((2, per_group, 8, 128), jnp.float32),
                dma((2,)),
                dma((2,)),
                dma((2,)),
                dma((3, 2)),
                dma((3, 2)),
                dma((2, reach, 4)),
                dma((2, reach, 4)),
                dma((groups,)),
                dma((groups,)),
                dma((2,)),
                dma((2,)),
            ],
            compiler_params=pltpu.CompilerParams(
                collective_id=0, has_side_effects=True, vmem_limit_bytes=32 * 1024 * 1024
            ),
        )(
            layer_slot,
            jnp.transpose(query_grads, (1, 0, 2)),
            out_basis,
            in_basis,
            eigen_scale,
            jnp.transpose(train_grads, (1, 0, 2)),
        )

    return jax.shard_map(
        on_device,
        mesh=mesh,
        in_specs=(
            P("shard", "layer", None),
            P("layer", None, None),
            P("layer", None, None),
            P("layer", None, None),
            P("layer"),
            P("shard", "layer", None),
        ),
        out_specs=P("layer", "shard"),
        check_vma=False,
    )
```

time: 332 us -> 62.5 us (0.19); the launches traced: 325 us -> 62.2 us
  waiting for transfers between devices: 105 us -> 0 us
  matrix products: 65.7 us -> 0 us
  local copies, waits for them, and re-layouts: 71.3 us -> 5.95 us
  Pallas kernels: 0 us -> 56.3 us
  blocking collectives: 53.8 us -> 0 us
  other arithmetic: 14.8 us -> 0 us
  between operations: 14.7 us -> 0.02 us
    all_gather x1 -> x0, waiting for transfers between devices: 105 us -> none  [on_device(): gathered = lax.all_gather(query_grads, 'shard', axis=0, tiled=True)]
    dot_general x14 -> x0, matrix products: 65.7 us -> none  [the longest x3 25.3 us: precondition_layer(): back = jnp.einsum('ab,nbd->nad', left_basis, rotated, precision=high)]
    pallas_call x0 -> x1, Pallas kernels: none -> 56.3 us  [on_device(): pl.pallas_call(functools.partial(kernel, ring, groups), out_shape=jax.Sha...]
    unnamed x1 -> x0, blocking collectives: 53.8 us -> none
    convert_element_type x3 -> x0, local copies, waits for them, and re-layouts: 16.9 us -> none  [precondition_all(): pieces.append(result.reshape(count, width).astype(jnp.bfloat16))]
    reshape x3 -> x0, local copies, waits for them, and re-layouts: 15.1 us -> none  [precondition_all(): queries[:, layer_index].astype(jnp.float32).reshape(count, side, side)]
    transpose x3 -> x0, local copies, waits for them, and re-layouts: 13.5 us -> none  [precondition_layer(): back = jnp.einsum('ab,nbd->nad', left_basis, rotated, precision=high)]
    reduce_sum x1 -> x0, other arithmetic: 12.6 us -> none  [on_device(): partial_norm = jnp.sum(wide * wide, axis=(1, 2))]
  transfers between devices with their start and end apart: 1 -> 0, of which waited for: 1 -> 0; matrix products, arithmetic and copies ran while one was open for 1% -> 0% of each run, Pallas kernels for 0% -> 0%
where the time goes in v1:
time: 62.5 us; the launch traced here: 62.2 us
  Pallas kernels  56.3 us (90%)
  local copies, waits for them, and re-layouts  5.95 us (10%)
    pallas_call x1, Pallas kernels, on_device(): pl.pallas_call(functools.partial(kernel, ring, groups), out_shape=jax.Sha...  56.3 us
    unnamed x13, local copies, waits for them, and re-layouts  5.95 us

profile of v1, /device:TPU:1, one launch (start us, length us, event | category | flops | bytes accessed | tf_op | source)
XLA Modules:
  0.0 62.2 jit_solution(1976256773855486125)
XLA Ops:
  0.0 0.0 copy-start.5
  0.0 0.7 %copy-done.5 = s32[3]{0:T(128)S(1)} copy-done((s32[3]{0:T(128)S(1)}, s32[3]{0:T(128)}, u32[]{:S(2)}) %copy-start.5) | copy-done | bytes 36
  0.7 0.0 copy-start
  0.7 1.1 %copy-done = bf16[32,3,4096]{2,0,1:T(8,128)(2,1)S(1)} copy-done((bf16[32,3,4096]{2,0,1:T(8,128)(2,1)S(1)}, bf16[32,3,4096]{2,0,1:T(8,128)(2,1)}, u32[]{:S(2)}) %copy-start) | copy-done | bytes 786456
  1.8 0.0 copy-start.1
  1.8 0.9 %copy-done.1 = bf16[4,3,4096]{2,0,1:T(4,128)(2,1)S(1)} copy-done((bf16[4,3,4096]{2,0,1:T(4,128)(2,1)S(1)}, bf16[4,3,4096]{2,0,1:T(4,128)(2,1)}, u32[]{:S(2)}) %copy-start.1) | copy-done | bytes 98328
  2.7 0.0 copy-start.2
  2.7 0.9 %copy-done.2 = f32[3,64,64]{2,1,0:T(8,128)S(1)} copy-done((f32[3,64,64]{2,1,0:T(8,128)S(1)}, f32[3,64,64]{2,1,0:T(8,128)}, u32[]{:S(2)}) %copy-start.2) | copy-done | bytes 49176
  3.6 0.0 copy-start.3
  3.6 0.9 %copy-done.3 = f32[3,64,64]{2,1,0:T(8,128)S(1)} copy-done((f32[3,64,64]{2,1,0:T(8,128)S(1)}, f32[3,64,64]{2,1,0:T(8,128)}, u32[]{:S(2)}) %copy-start.3) | copy-done | bytes 49176
  4.5 0.0 copy-start.4
  4.5 0.9 %copy-done.4 = f32[3,64,64]{2,1,0:T(8,128)S(1)} copy-done((f32[3,64,64]{2,1,0:T(8,128)S(1)}, f32[3,64,64]{2,1,0:T(8,128)}, u32[]{:S(2)}) %copy-start.4) | copy-done | bytes 49176
  5.4 56.3 %shard_map.64 = f32[8,32]{1,0:T(8,128)S(1)} custom-call(s32[3]{0:T(128)S(1)} %copy-done.5, bf16[3,4,4096]{2,1,0:T(4,128)(2,1)S(1)} %bitcast.3, f32[3,64,64]{2,1,0:T(8,128)S(1)} %copy-done.2, f32[3,64,64]{2,1,0:T(8,128)S(1)} %copy-done.3, f32[3,64,64]{2,1,0:T(8,128)S(1)} %copy-done.4, bf16[3,32,4096]{2,1,0:T(8,128)(2,1)S(1)} %bitcast.2), custom_call_target="tpu_custom_call" | custom-call | tf_op jit(solution)/shard_map/pallas_call | solution.py:326
  61.7 0.6 copy.8
Async XLA Ops:
  0.0 0.7 %copy-start.5 = (s32[3]{0:T(128)S(1)}, s32[3]{0:T(128)}, u32[]{:S(2)}) copy-start(s32[3]{0:T(128)} %slot_ref.1) | copy-start | bytes 40
  0.7 1.1 %copy-start = (bf16[32,3,4096]{2,0,1:T(8,128)(2,1)S(1)}, bf16[32,3,4096]{2,0,1:T(8,128)(2,1)}, u32[]{:S(2)}) copy-start(bf16[32,3,4096]{2,0,1:T(8,128)(2,1)} %param.11) | copy-start | bytes 2359300
  1.8 0.9 %copy-start.1 = (bf16[4,3,4096]{2,0,1:T(4,128)(2,1)S(1)}, bf16[4,3,4096]{2,0,1:T(4,128)(2,1)}, u32[]{:S(2)}) copy-start(bf16[4,3,4096]{2,0,1:T(4,128)(2,1)} %param.6) | copy-start | bytes 294916
  2.7 0.9 %copy-start.2 = (f32[3,64,64]{2,1,0:T(8,128)S(1)}, f32[3,64,64]{2,1,0:T(8,128)}, u32[]{:S(2)}) copy-start(f32[3,64,64]{2,1,0:T(8,128)} %s_ref.1) | copy-start | bytes 147460
  3.6 0.9 %copy-start.3 = (f32[3,64,64]{2,1,0:T(8,128)S(1)}, f32[3,64,64]{2,1,0:T(8,128)}, u32[]{:S(2)}) copy-start(f32[3,64,64]{2,1,0:T(8,128)} %a_ref.1) | copy-start | bytes 147460
  4.5 0.9 %copy-start.4 = (f32[3,64,64]{2,1,0:T(8,128)S(1)}, f32[3,64,64]{2,1,0:T(8,128)}, u32[]{:S(2)}) copy-start(f32[3,64,64]{2,1,0:T(8,128)} %e_ref.1) | copy-start | bytes 147460

commit v2 on v1

v2 whole, which is shorter than its diff:
```python
import functools

import jax
import jax.numpy as jnp
from jax import lax
from jax.experimental import pallas as pl
from jax.experimental.pallas import tpu as pltpu
from jax.sharding import PartitionSpec as P

DAMPING = 0.05
EPSILON = 1e-06
MESH = pl.DeviceIdType.MESH
COLUMNS = 4
OWN, FIRST, SECOND, ACROSS = range(4)
NEAR = (2, -2, 1, -1)
VMEM_BYTES = 63 * 1024 * 1024


def precondition_slot(index, slot, q_ref, s_ref, a_ref, e_ref, rows_ref, turned_ref, blocks_ref):
    high = lax.Precision.HIGHEST
    side = s_ref.shape[1]
    width = q_ref.shape[2]
    pieces = width // 128
    quarter = pieces // 8
    queries = q_ref[index].astype(jnp.float32)
    for piece in range(pieces):
        rows_ref[slot, 4 * piece : 4 * piece + 4, :] = queries[:, 128 * piece : 128 * (piece + 1)]
    count = side // 4
    basis = jnp.concatenate(
        [s_ref[index, pl.ds(2 * parity + half, count, stride=4), :] for half in range(2) for parity in range(2)], axis=0
    )
    right = a_ref[index]
    scale = e_ref[index] + DAMPING
    stacked = []
    for n in range(4):
        halves = [rows_ref[slot, pl.ds(4 * parity + n, count, stride=8), :] for parity in range(2)]
        both = jnp.concatenate(halves, axis=0)
        stacked.append(jnp.concatenate([both[:, :side], both[:, side:]], axis=0))
    stacked = jnp.concatenate(stacked, axis=0)
    stacked = lax.dot_general(stacked, right, (((1,), (0,)), ((), ())), precision=high, preferred_element_type=jnp.float32)
    wide = jnp.concatenate([stacked[side * n : side * (n + 1)] for n in range(4)], axis=1)
    wide = lax.dot_general(basis.T, wide, (((1,), (0,)), ((), ())), precision=high, preferred_element_type=jnp.float32)
    wide = wide / jnp.concatenate([scale] * 4, axis=1)
    wide = lax.dot_general(basis, wide, (((1,), (0,)), ((), ())), precision=high, preferred_element_type=jnp.float32)
    stacked = jnp.concatenate([wide[:, side * n : side * (n + 1)] for n in range(4)], axis=0)
    stacked = lax.dot_general(stacked, right, (((1,), (1,)), ((), ())), precision=high, preferred_element_type=jnp.float32)
    for n in range(4):
        block = stacked[side * n : side * (n + 1)]
        lanes = jnp.concatenate([block[: side // 2], block[side // 2 :]], axis=1)
        for parity in range(2):
            turned_ref[slot, parity, pl.ds(n, count, stride=4), :] = lanes[count * parity : count * (parity + 1)]
    for parity in range(2):
        for part in range(4):
            blocks_ref[part, :, 256 * slot + 128 * parity : 256 * slot + 128 * (parity + 1)] = turned_ref[
                slot, parity, 16 * part : 16 * (part + 1), :
            ].astype(jnp.bfloat16)


def kernel(
    ring,
    groups,
    slot_hbm,
    q_hbm,
    s_hbm,
    a_hbm,
    e_hbm,
    train_ref,
    out_ref,
    slot_ref,
    q_ref,
    s_ref,
    a_ref,
    e_ref,
    rows_ref,
    turned_ref,
    blocks_ref,
    train_part,
    gathered,
    total,
    squares,
    tiles,
    tiles_in,
    summed,
    summed_in,
    local_sem,
    t_send,
    t_recv,
    y_send,
    y_recv,
    near_send,
    near_recv,
    far_send,
    far_recv,
    r_send,
    r_recv,
    p_send,
    p_recv,
):
    shard = lax.axis_index("shard")
    group = lax.axis_index("layer")
    column = shard // ring
    level = lax.rem(shard, ring)
    slots = q_ref.shape[0]
    tile_count = tiles.shape[0]

    def at(col, lev):
        return col * ring + lev

    def shifted(by):
        return lax.rem(level + by + ring, ring)

    first = column + 1 - 2 * lax.rem(column, 2)
    second = 3 - column
    across = 3 - first
    columns = [column, first, second, across]

    def remote(src, dst, send, recv, to_shard, to_group):
        return pltpu.make_async_remote_copy(
            src_ref=src, dst_ref=dst, send_sem=send, recv_sem=recv, device_id=(to_shard, to_group), device_id_type=MESH
        )

    loads = []
    for i, (src, dst) in enumerate(
        [(q_hbm, q_ref), (a_hbm, a_ref), (s_hbm, s_ref), (e_hbm, e_ref), (slot_hbm, slot_ref)]
    ):
        copy = pltpu.make_async_copy(src, dst, local_sem.at[i])
        copy.start()
        loads.append(copy)

    span = train_ref.shape[2] // COLUMNS

    def quarter_of_train(quarter):
        return train_ref.at[:, :, pl.ds(pl.multiple_of(quarter * span, 128), span)]

    keep = pltpu.make_async_copy(quarter_of_train(column), train_part.at[OWN], local_sem.at[len(loads)])
    keep.start()

    barrier = pltpu.get_barrier_semaphore()
    partners = [(at(column, shifted(by)), group) for by in NEAR]
    partners += [(at(c, level), group) for c in columns[1:]]
    partners += [(shard, lax.rem(group + d, groups)) for d in range(1, groups)]
    for who in partners:
        pl.semaphore_signal(barrier, inc=1, device_id=who, device_id_type=MESH)
    pl.semaphore_wait(barrier, len(partners))

    train_copies = []
    for who in (FIRST, SECOND, ACROSS):
        copy = remote(
            quarter_of_train(columns[who]), train_part.at[who], t_send.at[who], t_recv.at[who], at(columns[who], level), group
        )
        copy.start()
        train_copies.append(copy)

    for copy in loads:
        copy.wait()
    for slot in range(slots):
        index = lax.rem(slot_ref[slot], slots)
        precondition_slot(index, slot, q_ref, s_ref, a_ref, e_ref, rows_ref, turned_ref, blocks_ref)

    column_copies = []
    for who in (FIRST, SECOND, ACROSS):
        copy = remote(
            blocks_ref.at[columns[who]],
            gathered.at[column, level],
            y_send.at[who],
            y_recv.at[who],
            at(columns[who], level),
            group,
        )
        copy.start()
        column_copies.append(copy)
    gathered[column, level] = blocks_ref[column]

    def block_of(who, by):
        return gathered.at[columns[who], shifted(by)]

    near_copies, far_copies = [], []
    for who in range(COLUMNS):
        if who != OWN:
            remote(
                blocks_ref.at[0], block_of(who, 0), y_send.at[who], y_recv.at[who], at(columns[who], level), group
            ).wait_recv()
        for i, by in enumerate(NEAR):
            copy = remote(
                block_of(who, 0), block_of(who, 0), near_send.at[i, who], near_recv.at[i, who], at(column, shifted(by)), group
            )
            copy.start()
            near_copies.append(copy)

    def near_arrive(i, who):
        block = block_of(who, -NEAR[i])
        remote(block, block, near_send.at[i, who], near_recv.at[i, who], at(column, shifted(NEAR[i])), group).wait_recv()

    far = [(0, -2, 1, range(4)), (1, 2, -1, range(4)), (2, -2, 2, (0, 1)), (3, 2, -2, (2, 3))]
    for who in range(COLUMNS):
        for i, by in enumerate(NEAR[:2]):
            near_arrive(i, who)
            for row, source, on, which in far:
                if source == -by and who in which:
                    block = block_of(who, source)
                    copy = remote(
                        block, block, far_send.at[row, who], far_recv.at[row, who], at(column, shifted(on)), group
                    )
                    copy.start()
                    far_copies.append(copy)
    for who in range(COLUMNS):
        for i in range(2, len(NEAR)):
            near_arrive(i, who)

    def multiply(levels):
        left = [gathered[:, pl.ds(lev, 1)].reshape(16 * COLUMNS, 256 * slots) for lev in levels]
        left = jnp.concatenate(left, axis=0) if len(left) > 1 else left[0]
        wide = left.astype(jnp.float32)
        wide = wide * wide
        norm = wide[:, :128]
        for piece in range(1, 2 * slots):
            norm = norm + wide[:, 128 * piece : 128 * (piece + 1)]
        row = lax.broadcasted_iota(jnp.int32, (16, 128), 0) // 4
        lane = lax.broadcasted_iota(jnp.int32, (16, 128), 1) // 32
        same = row == lane
        for who in range(COLUMNS):
            product = None
            for slot in range(slots):
                right = jnp.concatenate(
                    [train_part[who, slot, :, 256 * sub : 256 * (sub + 1)] for sub in range(4)], axis=0
                )
                term = lax.dot_general(
                    left[:, 256 * slot : 256 * (slot + 1)],
                    right,
                    (((1,), (1,)), ((), ())),
                    preferred_element_type=jnp.float32,
                )
                product = term if product is None else product + term
            for at_level, lev in enumerate(levels):
                for col in range(COLUMNS):
                    start = 16 * (COLUMNS * at_level + col)
                    kept = jnp.where(same, product[start : start + 16], 0.0)
                    total[col, lev, :, 128 * who : 128 * (who + 1)] = kept[:8] + kept[8:]
        for at_level, lev in enumerate(levels):
            for col in range(COLUMNS):
                start = 16 * (COLUMNS * at_level + col)
                squares[col, lev] = norm[start : start + 8] + norm[start + 8 : start + 16]

    keep.wait()
    for copy in train_copies:
        copy.wait_recv()
    multiply([level] + [shifted(by) for by in NEAR])
    for row, source, on, which in far:
        for who in which:
            block = block_of(who, source - on)
            remote(block, block, far_send.at[row, who], far_recv.at[row, who], at(column, shifted(on)), group).wait_recv()
    multiply([shifted(by) for by in (3, 4, 5)])

    row = lax.broadcasted_iota(jnp.int32, (8, 128), 0)
    lane = lax.broadcasted_iota(jnp.int32, (8, 128), 1) // 32

    def fold(value):
        value = value + pltpu.roll(value, 64, 1)
        return value + pltpu.roll(value, 32, 1)

    per_column = ring // 2

    def make_tile(tile, carry):
        col, pair_of_levels = tile // per_column, lax.rem(tile, per_column)

        def rows_of(ref, lanes):
            even, odd = (ref[col, 2 * pair_of_levels + k, :, lanes] for k in range(2))
            even = even + pltpu.roll(even, 4, 0)
            odd = odd + pltpu.roll(odd, 4, 0)
            return jnp.where(row < 4, even, odd)

        value = fold(rows_of(total, slice(0, 128)))
        for who in range(1, COLUMNS):
            value = jnp.where(lane < who, value, fold(rows_of(total, slice(128 * who, 128 * (who + 1)))))
        norm = jnp.sum(rows_of(squares, slice(0, 128)), axis=1, keepdims=True)
        tiles[tile, :, :128] = value
        tiles[tile, :, 128:] = jnp.broadcast_to(norm, value.shape)
        return carry

    lax.fori_loop(0, tile_count, make_tile, 0)

    per_group = tile_count // groups
    group_copies = []
    for d in range(1, groups):
        to = lax.rem(group + d, groups)
        copy = remote(tiles.at[pl.ds(to * per_group, per_group)], tiles_in.at[d], r_send.at[d], r_recv.at[d], shard, to)
        copy.start()
        group_copies.append(copy)
    answer = tiles[pl.ds(group * per_group, per_group)]
    for copy in group_copies:
        copy.wait_recv()
    for d in range(1, groups):
        answer = answer + tiles_in[d]
    summed[...] = answer
    pair_copies = []
    for who in (FIRST, SECOND, ACROSS):
        copy = remote(summed, summed_in.at[who], p_send.at[who], p_recv.at[who], at(columns[who], level), group)
        copy.start()
        pair_copies.append(copy)
    for copy in pair_copies:
        copy.wait_recv()
    raw, norm = answer[:, :, :32], answer[:, :, 128:129]
    for who in (FIRST, SECOND, ACROSS):
        raw = raw + summed_in[who, :, :, 32 * who : 32 * (who + 1)]
        norm = norm + summed_in[who, :, :, 128:129]
    out_ref[...] = (raw / jnp.sqrt(norm + EPSILON)).reshape(out_ref.shape)

    for copy in train_copies + column_copies + near_copies + far_copies + group_copies + pair_copies:
        copy.wait_send()


def solution(mesh):
    shards, groups = mesh.shape["shard"], mesh.shape["layer"]
    ring = shards // COLUMNS

    def on_device(query_grads, out_basis, in_basis, eigen_scale, layer_slot, train_grads):
        local, slots, width = query_grads.shape
        side = out_basis.shape[1]
        rows = train_grads.shape[0]
        tile_count = local * shards // 8
        per_group = tile_count // groups
        dma = pltpu.SemaphoreType.DMA
        return pl.pallas_call(
            functools.partial(kernel, ring, groups),
            out_shape=jax.ShapeDtypeStruct((8 * per_group, rows), jnp.float32),
            in_specs=[pl.BlockSpec(memory_space=pl.ANY)] * 6,
            out_specs=pl.BlockSpec(memory_space=pltpu.VMEM),
            scratch_shapes=[
                pltpu.SMEM((slots,), jnp.int32),
                pltpu.VMEM((slots, local, width), jnp.bfloat16),
                pltpu.VMEM((slots, side, side), jnp.float32),
                pltpu.VMEM((slots, side, side), jnp.float32),
                pltpu.VMEM((slots, side, side), jnp.float32),
                pltpu.VMEM((slots, local * width // 128, 128), jnp.float32),
                pltpu.VMEM((slots, 2, local * width // 256, 128), jnp.float32),
                pltpu.VMEM((COLUMNS, 16, 256 * slots), jnp.bfloat16),
                pltpu.VMEM((COLUMNS, slots, rows, width // COLUMNS), jnp.bfloat16),
                pltpu.VMEM((COLUMNS, ring, 16, 256 * slots), jnp.bfloat16),
                pltpu.VMEM((COLUMNS, ring, 8, 128 * COLUMNS), jnp.float32),
                pltpu.VMEM((COLUMNS, ring, 8, 128), jnp.float32),
                pltpu.VMEM((tile_count, 8, 256), jnp.float32),
                pltpu.VMEM((groups, per_group, 8, 256), jnp.float32),
                pltpu.VMEM((per_group, 8, 256), jnp.float32),
                pltpu.VMEM((COLUMNS, per_group, 8, 256), jnp.float32),
                dma((6,)),
                dma((COLUMNS,)),
                dma((COLUMNS,)),
                dma((COLUMNS,)),
                dma((COLUMNS,)),
                dma((4, COLUMNS)),
                dma((4, COLUMNS)),
                dma((4, COLUMNS)),
                dma((4, COLUMNS)),
                dma((groups,)),
                dma((groups,)),
                dma((COLUMNS,)),
                dma((COLUMNS,)),
            ],
            compiler_params=pltpu.CompilerParams(
                collective_id=0, has_side_effects=True, vmem_limit_bytes=VMEM_BYTES
            ),
        )(
            layer_slot,
            jnp.transpose(query_grads, (1, 0, 2)),
            out_basis,
            in_basis,
            eigen_scale,
            jnp.transpose(train_grads, (1, 0, 2)),
        )

    return jax.shard_map(
        on_device,
        mesh=mesh,
        in_specs=(
            P("shard", "layer", None),
            P("layer", None, None),
            P("layer", None, None),
            P("layer", None, None),
            P("layer"),
            P("shard", "layer", None),
        ),
        out_specs=P("layer", "shard"),
        check_vma=False,
    )
```

time: 62.5 us -> 60.3 us (0.965)
  local copies, waits for them, and re-layouts: 5.95 us -> 1.28 us
  Pallas kernels: 56.3 us -> 58.9 us
    unnamed x13 -> x1, local copies, waits for them, and re-layouts: 5.95 us -> 1.28 us
    pallas_call x1, Pallas kernels: 56.3 us -> 58.9 us  [on_device(): pl.pallas_call(functools.partial(kernel, ring, groups), out_shape=jax.Sha...]
where the time goes in v2:
time: 60.3 us; the launch traced here: 60.2 us
  Pallas kernels  58.9 us (98%)
  local copies, waits for them, and re-layouts  1.28 us (2%)
    pallas_call x1, Pallas kernels, on_device(): pl.pallas_call(functools.partial(kernel, ring, groups), out_shape=jax.Sha...  58.9 us
    unnamed x1, local copies, waits for them, and re-layouts  1.28 us

profile of v2, /device:TPU:1, one launch (start us, length us, event | category | flops | bytes accessed | tf_op | source)
XLA Modules:
  0.0 60.2 jit_solution(16790068209568704674)
XLA Ops:
  0.0 58.9 %shard_map.64 = f32[8,32]{1,0:T(8,128)} custom-call(s32[3]{0:T(128)} %slot_hbm.1, bf16[3,4,4096]{2,1,0:T(4,128)(2,1)} %bitcast.3, f32[3,64,64]{2,1,0:T(8,128)} %s_hbm.1, f32[3,64,64]{2,1,0:T(8,128)} %a_hbm.1, f32[3,64,64]{2,1,0:T(8,128)} %e_hbm.1, bf16[3,32,4096]{2,1,0:T(8,128)(2,1)} %bitcast.2), custom_call_target="tpu_custom_call" | custom-call | tf_op jit(solution)/shard_map/pallas_call | solution.py:323
  58.9 1.3 %copy.8 = f32[8,32]{1,0:T(8,128)} copy(f32[8,32]{1,0:T(8,128)} %shard_map.64) | data formatting | bytes 2048

commit v3 on v2

--- a/solution.py
+++ b/solution.py
@@ -138,18 +138,33 @@
     barrier = pltpu.get_barrier_semaphore()
     partners = [(at(column, shifted(by)), group) for by in NEAR]
     partners += [(at(c, level), group) for c in columns[1:]]
-    partners += [(shard, lax.rem(group + d, groups)) for d in range(1, groups)]
     for who in partners:
         pl.semaphore_signal(barrier, inc=1, device_id=who, device_id_type=MESH)
-    pl.semaphore_wait(barrier, len(partners))
+
+    def greet(d, carry):
+        pl.semaphore_signal(barrier, inc=1, device_id=(shard, lax.rem(group + d, groups)), device_id_type=MESH)
+        return carry
+
+    lax.fori_loop(1, groups, greet, 0)
+    pl.semaphore_wait(barrier, len(partners) + groups - 1)
 
     train_copies = []
-    for who in (FIRST, SECOND, ACROSS):
+
+    def send_train(who, piece):
+        lots = pl.ds(0, 1) if piece == 0 else pl.ds(1, slots - 1)
         copy = remote(
-            quarter_of_train(columns[who]), train_part.at[who], t_send.at[who], t_recv.at[who], at(columns[who], level), group
+            quarter_of_train(columns[who]).at[lots],
+            train_part.at[who, lots],
+            t_send.at[who, piece],
+            t_recv.at[who, piece],
+            at(columns[who], level),
+            group,
         )
         copy.start()
         train_copies.append(copy)
+
+    for who in (FIRST, SECOND):
+        send_train(who, 0)
 
     for copy in loads:
         copy.wait()
@@ -170,6 +185,8 @@
         copy.start()
         column_copies.append(copy)
     gathered[column, level] = blocks_ref[column]
+    for who, piece in ((FIRST, 1), (SECOND, 1), (ACROSS, 0), (ACROSS, 1)):
+        send_train(who, piece)
 
     def block_of(who, by):
         return gathered.at[columns[who], shifted(by)]
@@ -280,17 +297,23 @@
     lax.fori_loop(0, tile_count, make_tile, 0)
 
     per_group = tile_count // groups
-    group_copies = []
-    for d in range(1, groups):
+
+    def group_copy(d):
         to = lax.rem(group + d, groups)
-        copy = remote(tiles.at[pl.ds(to * per_group, per_group)], tiles_in.at[d], r_send.at[d], r_recv.at[d], shard, to)
-        copy.start()
-        group_copies.append(copy)
-    answer = tiles[pl.ds(group * per_group, per_group)]
-    for copy in group_copies:
-        copy.wait_recv()
-    for d in range(1, groups):
-        answer = answer + tiles_in[d]
+        return remote(
+            tiles.at[pl.ds(to * per_group, per_group)], tiles_in.at[d], r_send.at[d], r_recv.at[d], shard, to
+        )
+
+    def send_tile(d, carry):
+        group_copy(d).start()
+        return carry
+
+    def add_tile(d, answer):
+        group_copy(d).wait_recv()
+        return answer + tiles_in[d]
+
+    lax.fori_loop(1, groups, send_tile, 0)
+    answer = lax.fori_loop(1, groups, add_tile, tiles[pl.ds(group * per_group, per_group)])
     summed[...] = answer
     pair_copies = []
     for who in (FIRST, SECOND, ACROSS):
@@ -305,7 +328,12 @@
         norm = norm + summed_in[who, :, :, 128:129]
     out_ref[...] = (raw / jnp.sqrt(norm + EPSILON)).reshape(out_ref.shape)
 
-    for copy in train_copies + column_copies + near_copies + far_copies + group_copies + pair_copies:
+    def tile_sent(d, carry):
+        group_copy(d).wait_send()
+        return carry
+
+    lax.fori_loop(1, groups, tile_sent, 0)
+    for copy in train_copies + column_copies + near_copies + far_copies + pair_copies:
         copy.wait_send()
 
 
@@ -343,8 +371,8 @@
                 pltpu.VMEM((per_group, 8, 256), jnp.float32),
                 pltpu.VMEM((COLUMNS, per_group, 8, 256), jnp.float32),
                 dma((6,)),
-                dma((COLUMNS,)),
-                dma((COLUMNS,)),
+                dma((COLUMNS, 2)),
+                dma((COLUMNS, 2)),
                 dma((COLUMNS,)),
                 dma((COLUMNS,)),
                 dma((4, COLUMNS)),

time: 60.3 us -> 50.7 us (0.84)
  Pallas kernels: 58.9 us -> 49.2 us
    pallas_call x1, Pallas kernels: 58.9 us -> 49.2 us  [on_device(): pl.pallas_call(functools.partial(kernel, ring, groups), out_shape=jax.Sha...]
where the time goes in v3:
time: 50.7 us; the launch traced here: 50.5 us
  Pallas kernels  49.2 us (97%)
  local copies, waits for them, and re-layouts  1.28 us (3%)
    pallas_call x1, Pallas kernels, on_device(): pl.pallas_call(functools.partial(kernel, ring, groups), out_shape=jax.Sha...  49.2 us
    unnamed x1, local copies, waits for them, and re-layouts  1.28 us

profile of v3, /device:TPU:1, one launch (start us, length us, event | category | flops | bytes accessed | tf_op | source)
XLA Modules:
  0.0 50.5 jit_solution(10279748703818852514)
XLA Ops:
  0.0 49.2 %shard_map.64 = f32[8,32]{1,0:T(8,128)} custom-call(s32[3]{0:T(128)} %slot_hbm.1, bf16[3,4,4096]{2,1,0:T(4,128)(2,1)} %bitcast.3, f32[3,64,64]{2,1,0:T(8,128)} %s_hbm.1, f32[3,64,64]{2,1,0:T(8,128)} %a_hbm.1, f32[3,64,64]{2,1,0:T(8,128)} %e_hbm.1, bf16[3,32,4096]{2,1,0:T(8,128)(2,1)} %bitcast.2), custom_call_target="tpu_custom_call" | custom-call | tf_op jit(solution)/shard_map/pallas_call | solution.py:351
  49.3 1.3 %copy.8 = f32[8,32]{1,0:T(8,128)} copy(f32[8,32]{1,0:T(8,128)} %shard_map.64) | data formatting | bytes 2048

commit v4 on v0

v4 whole, which is shorter than its diff:
```python
import functools

import jax
import jax.numpy as jnp
from jax import lax
from jax.experimental import pallas as pl
from jax.experimental.pallas import tpu as pltpu
from jax.sharding import PartitionSpec as P

DAMPING = 0.05
EPSILON = 1e-06
MESH = pl.DeviceIdType.MESH
PARTS = 8
COLUMNS = 4
OWN, FIRST, SECOND, ACROSS = range(4)
NEAR = (2, -2, 1, -1)
LOTS = (slice(0, 1), slice(1, 4), slice(0, 2), slice(2, 4))
VMEM_BYTES = 40 * 1024 * 1024


def split(value):
    top = value.astype(jnp.bfloat16)
    return top, (value - top.astype(jnp.float32)).astype(jnp.bfloat16)


def product(left, right, contract):
    dims = (contract, ((), ()))
    total = None
    for i, a in enumerate(left):
        for b in right[: len(right) - i]:
            term = lax.dot_general(a, b, dims, preferred_element_type=jnp.float32)
            total = term if total is None else total + term
    return total


def precondition_slot(index, slot, q_ref, s_ref, a_ref, e_ref, rows_ref, turned_ref, blocks_ref):
    side = s_ref.shape[1]
    width = q_ref.shape[2]
    pieces = width // 128
    half = side // 2
    queries = q_ref[index].astype(jnp.float32)
    for piece in range(pieces):
        rows_ref[slot, 4 * piece : 4 * piece + 4, :] = queries[:, 128 * piece : 128 * (piece + 1)]
    basis = jnp.concatenate([s_ref[index, pl.ds(parity, half, stride=2), :] for parity in range(2)], axis=0)
    right = split(a_ref[index])
    scale = e_ref[index] + DAMPING
    stacked = []
    for n in range(4):
        both = rows_ref[slot, pl.ds(n, half, stride=4), :]
        stacked.append(jnp.concatenate([both[:, :side], both[:, side:]], axis=0))
    stacked = jnp.concatenate(stacked, axis=0)
    stacked = product((stacked.astype(jnp.bfloat16),), right, ((1,), (0,)))
    wide = jnp.concatenate([stacked[side * n : side * (n + 1)] for n in range(4)], axis=1)
    wide = product(split(basis.T), split(wide), ((1,), (0,)))
    wide = wide / jnp.concatenate([scale] * 4, axis=1)
    wide = product(split(basis), split(wide), ((1,), (0,)))
    stacked = jnp.concatenate([wide[:, side * n : side * (n + 1)] for n in range(4)], axis=0)
    stacked = product(split(stacked), right, ((1,), (1,)))
    for n in range(4):
        block = stacked[side * n : side * (n + 1)]
        turned_ref[slot, pl.ds(n, half, stride=4), :] = jnp.concatenate([block[:half], block[half:]], axis=1)
    for part in range(PARTS):
        blocks_ref[part, :, 128 * slot : 128 * (slot + 1)] = turned_ref[slot, 16 * part : 16 * (part + 1), :].astype(
            jnp.bfloat16
        )


def kernel(
    ring,
    groups,
    slot_hbm,
    q_hbm,
    s_hbm,
    a_hbm,
    e_hbm,
    train_ref,
    out_ref,
    slot_ref,
    q_ref,
    s_ref,
    a_ref,
    e_ref,
    rows_ref,
    turned_ref,
    blocks_ref,
    train_part,
    gathered,
    tiles,
    tiles_in,
    pair_out,
    pair_in,
    local_sem,
    t_send,
    t_recv,
    q_send,
    q_recv,
    near_send,
    near_recv,
    far_send,
    far_recv,
    across_send,
    across_recv,
    r_send,
    r_recv,
    p_send,
    p_recv,
):
    shard = lax.axis_index("shard")
    group = lax.axis_index("layer")
    core = lax.rem(group, 2)
    column = shard // ring
    level = lax.rem(shard, ring)
    slots = q_ref.shape[0]
    tile_count = tiles.shape[0]

    def at(col, lev):
        return col * ring + lev

    def shifted(by):
        return lax.rem(level + by + ring, ring)

    first = column + 1 - 2 * lax.rem(column, 2)
    second = 3 - column
    across = 3 - first
    columns = [column, first, second, across]

    def remote(src, dst, send, recv, to_shard, to_group=group):
        return pltpu.make_async_remote_copy(
            src_ref=src, dst_ref=dst, send_sem=send, recv_sem=recv, device_id=(to_shard, to_group), device_id_type=MESH
        )

    barrier = pltpu.get_barrier_semaphore()
    partners = [(at(column, shifted(by)), group) for by in range(1, ring)]
    partners += [(at(c, level), group) for c in columns[1:]]
    for who in partners:
        pl.semaphore_signal(barrier, inc=1, device_id=who, device_id_type=MESH)

    def greet(d, carry):
        pl.semaphore_signal(barrier, inc=1, device_id=(shard, lax.rem(group + d, groups)), device_id_type=MESH)
        return carry

    lax.fori_loop(1, groups, greet, 0)
    loads = []
    for i, (src, dst) in enumerate(
        [(q_hbm, q_ref), (a_hbm, a_ref), (s_hbm, s_ref), (e_hbm, e_ref), (slot_hbm, slot_ref)]
    ):
        copy = pltpu.make_async_copy(src, dst, local_sem.at[i])
        copy.start()
        loads.append(copy)

    pl.semaphore_wait(barrier, len(partners) + groups - 1)

    span = train_ref.shape[2] // PARTS

    def part_of_train(part):
        return train_ref.at[:, :, pl.ds(pl.multiple_of(part * span, 128), span)]

    def train_to_column(who, half):
        i = 2 * who + half
        return remote(
            part_of_train(2 * columns[who] + half), train_part.at[i], t_send.at[i], t_recv.at[i], at(columns[who], level)
        )

    def train_to_level(i):
        to = shifted(-i)
        return remote(part_of_train(to), train_part.at[i], t_send.at[i], t_recv.at[i], at(column, to))

    def keep_for_column(half):
        return pltpu.make_async_copy(
            part_of_train(2 * column + half), train_part.at[half], local_sem.at[len(loads) + half]
        )

    def keep_for_level():
        return pltpu.make_async_copy(part_of_train(level), train_part.at[0], local_sem.at[len(loads)])

    @pl.when(core == 0)
    def _():
        for who in (FIRST, SECOND):
            train_to_column(who, 0).start()
        for half in range(2):
            keep_for_column(half).start()

    @pl.when(core == 1)
    def _():
        for i in (2, 6):
            train_to_level(i).start()
        keep_for_level().start()

    for copy in loads:
        copy.wait()
    for slot in range(slots):
        index = lax.rem(slot_ref[slot], slots)
        precondition_slot(index, slot, q_ref, s_ref, a_ref, e_ref, rows_ref, turned_ref, blocks_ref)

    @pl.when(core == 0)
    def _():
        def own_to_column(who):
            return remote(
                blocks_ref.at[pl.ds(2 * columns[who], 2)],
                gathered.at[:, who, level],
                q_send.at[who],
                q_recv.at[who],
                at(columns[who], level),
            )

        def block_of(lot, by):
            return gathered.at[:, LOTS[lot], shifted(by)]

        def near_copy(i, lot, source=0):
            block = block_of(lot, source)
            return remote(block, block, near_send.at[i, lot], near_recv.at[i, lot], at(column, shifted(NEAR[i])))

        for who in (FIRST, SECOND, ACROSS):
            own_to_column(who).start()
        for who in (FIRST, SECOND):
            train_to_column(who, 1).start()
        for half in range(2):
            gathered[half, OWN, level] = blocks_ref[2 * column + half]
        for i in range(len(NEAR)):
            near_copy(i, 0).start()
        for who in (FIRST, SECOND, ACROSS):
            own_to_column(who).wait_recv()
        for i in range(len(NEAR)):
            near_copy(i, 1).start()
        for half in range(2):
            train_to_column(ACROSS, half).start()

        def far_copy(row, lot, source, on):
            block = block_of(lot, source)
            return remote(block, block, far_send.at[row, lot], far_recv.at[row, lot], at(column, shifted(on)))

        far = [(0, 0, -2, 1), (1, 0, 2, -1), (0, 1, -2, 1), (1, 1, 2, -1), (2, 2, -2, 2), (3, 3, 2, -2)]
        for lot in range(2):
            for i in range(2):
                near_copy(i, lot, -NEAR[i]).wait_recv()
        for row, lot, source, on in far:
            far_copy(row, lot, source, on).start()
        for lot in range(2):
            for i in range(2, len(NEAR)):
                near_copy(i, lot, -NEAR[i]).wait_recv()
        for row, lot, source, on in far:
            far_copy(row, lot, source - on, on).wait_recv()
        for half in range(2):
            keep_for_column(half).wait()
            for who in (FIRST, SECOND, ACROSS):
                train_to_column(who, half).wait_recv()
        for half in range(2):
            for who in (FIRST, SECOND, ACROSS):
                train_to_column(who, half).wait_send()
        for who in (FIRST, SECOND, ACROSS):
            own_to_column(who).wait_send()
        for lot in range(2):
            for i in range(len(NEAR)):
                near_copy(i, lot).wait_send()
        for row, lot, source, on in far:
            far_copy(row, lot, source, on).wait_send()

    @pl.when(core == 1)
    def _():
        def own_to_level(i):
            to = shifted(-i)
            return remote(
                blocks_ref.at[to], gathered.at[0, OWN, level], q_send.at[i], q_recv.at[i], at(column, to)
            )

        def levels_to_column(who):
            return remote(
                gathered.at[0, OWN],
                gathered.at[0, who],
                across_send.at[who],
                across_recv.at[who],
                at(columns[who], level),
            )

        order = (4, 3, 5, 2, 6, 1, 7)
        for i in order:
            own_to_level(i).start()
        for i in (1, 7, 3, 5, 4):
            train_to_level(i).start()
        gathered[0, OWN, level] = blocks_ref[level]
        for i in order:
            remote(
                blocks_ref.at[0],
                gathered.at[0, OWN, shifted(i)],
                q_send.at[i],
                q_recv.at[i],
                at(column, shifted(-i)),
            ).wait_recv()
        for who in (ACROSS, FIRST, SECOND):
            levels_to_column(who).start()
        for who in (ACROSS, FIRST, SECOND):
            levels_to_column(who).wait_recv()
        keep_for_level().wait()
        for i in range(1, ring):
            train_to_level(i).wait_recv()
        for i in range(1, ring):
            train_to_level(i).wait_send()
            own_to_level(i).wait_send()
        for who in (ACROSS, FIRST, SECOND):
            levels_to_column(who).wait_send()

    count = COLUMNS * ring
    left = [gathered[part].reshape(16 * count, 128 * slots) for part in (0, 1 - core)]
    squares = [value.astype(jnp.float32) for value in left]
    squares = squares[0] * squares[0] + jnp.where(core == 0, squares[1] * squares[1], 0.0)
    norm = squares[:, :128]
    for slot in range(1, slots):
        norm = norm + squares[:, 128 * slot : 128 * (slot + 1)]

    row = lax.broadcasted_iota(jnp.int32, (tile_count, 8, 128), 1)
    lane = lax.broadcasted_iota(jnp.int32, (tile_count, 8, 128), 2) // 32
    same = lax.broadcasted_iota(jnp.int32, (count, 16, 128), 1) // 4 == (
        lax.broadcasted_iota(jnp.int32, (count, 16, 128), 2) // 32
    )

    def queries_of(value):
        value = value[:, :8] + value[:, 8:]
        value = (value + pltpu.roll(value, 4, 1)).reshape(tile_count, 2, 8, 128)
        return jnp.where(row < 4, value[:, 0], value[:, 1])

    low = jnp.zeros((tile_count, 8, 128), jnp.float32)
    high = low
    for i in range(PARTS):
        right = jnp.concatenate(
            [
                jnp.concatenate([train_part[i, slot, :, 128 * sub : 128 * (sub + 1)] for slot in range(slots)], axis=1)
                for sub in range(4)
            ],
            axis=0,
        )
        product = lax.dot_general(
            left[i % 2], right, (((1,), (1,)), ((), ())), preferred_element_type=jnp.float32
        ).reshape(count, 16, 128)
        value = queries_of(jnp.where(same, product, 0.0))
        value = value + pltpu.roll(value, 64, 2)
        value = value + pltpu.roll(value, 32, 2)
        low = low + jnp.where(lane == jnp.where(core == 0, i // 2, i), value, 0.0)
        if i >= 4:
            high = high + jnp.where(lane == i - 4, value, 0.0)
    norm = jnp.sum(queries_of(norm.reshape(count, 16, 128)), axis=2, keepdims=True)
    per_column = tile_count // COLUMNS
    for who in range(COLUMNS):
        place = pl.ds(columns[who] * per_column, per_column)
        some = slice(who * per_column, (who + 1) * per_column)
        tiles[place, :, :128] = low[some]
        tiles[place, :, 128:256] = high[some]
        tiles[place, :, 256:] = jnp.broadcast_to(norm[some], (per_column, 8, 128))

    per_group = tile_count // groups

    def group_copy(d):
        to = lax.rem(group + d, groups)
        return remote(
            tiles.at[pl.ds(to * per_group, per_group)], tiles_in.at[d], r_send.at[d], r_recv.at[d], shard, to
        )

    def send_tile(d, carry):
        group_copy(d).start()
        return carry

    lax.fori_loop(1, groups, send_tile, 0)
    sums = [tiles[pl.ds(group * per_group, per_group)], None]
    for d in range(1, groups):
        group_copy(d).wait_recv()
        sums[d % 2] = tiles_in[d] if sums[d % 2] is None else sums[d % 2] + tiles_in[d]
    by_column = jnp.where(core == 0, sums[0], sums[1])
    by_level = jnp.where(core == 0, sums[1], sums[0])

    scores_of = [by_column[:, :, :128]] * COLUMNS + [by_level[:, :, :128]] * 4 + [by_level[:, :, 128:256]] * 4
    squares_of = [by_column[:, :, 256:]] * COLUMNS + [by_level[:, :, 256:]] * ring
    is_score = lax.broadcasted_iota(jnp.int32, (per_group, 8, 128), 2) < 32

    def packed(j):
        turned = scores_of[j] if j % 4 == 0 else pltpu.roll(scores_of[j], 128 - 32 * (j % 4), 2)
        return jnp.where(is_score, turned, squares_of[j])

    def pair_copy(j):
        to = at(columns[j], level) if j < COLUMNS else at(column, shifted(j - COLUMNS))
        return remote(pair_out.at[j], pair_in.at[j], p_send.at[j], p_recv.at[j], to)

    others = [COLUMNS + i for i in (4, 3, 5)] + [ACROSS] + [COLUMNS + i for i in (2, 6)] + [FIRST, SECOND]
    others += [COLUMNS + i for i in (1, 7)]
    for j in others:
        pair_out[j] = packed(j)
        pair_copy(j).start()
    answer = packed(OWN) + packed(COLUMNS)
    for j in reversed(others):
        pair_copy(j).wait_recv()
        answer = answer + pair_in[j]
    out_ref[...] = (answer[:, :, :32] / jnp.sqrt(answer[:, :, 32:33] + EPSILON)).reshape(out_ref.shape)

    def tile_sent(d, carry):
        group_copy(d).wait_send()
        return carry

    lax.fori_loop(1, groups, tile_sent, 0)
    for j in others:
        pair_copy(j).wait_send()


def solution(mesh):
    shards, groups = mesh.shape["shard"], mesh.shape["layer"]
    ring = shards // COLUMNS

    def on_device(query_grads, out_basis, in_basis, eigen_scale, layer_slot, train_grads):
        local, slots, width = query_grads.shape
        side = out_basis.shape[1]
        rows = train_grads.shape[0]
        tile_count = local * shards // 8
        per_group = tile_count // groups
        dma = pltpu.SemaphoreType.DMA
        return pl.pallas_call(
            functools.partial(kernel, ring, groups),
            out_shape=jax.ShapeDtypeStruct((8 * per_group, rows), jnp.float32),
            in_specs=[pl.BlockSpec(memory_space=pl.ANY)] * 6,
            out_specs=pl.BlockSpec(memory_space=pltpu.VMEM),
            scratch_shapes=[
                pltpu.SMEM((slots,), jnp.int32),
                pltpu.VMEM((slots, local, width), jnp.bfloat16),
                pltpu.VMEM((slots, side, side), jnp.float32),
                pltpu.VMEM((slots, side, side), jnp.float32),
                pltpu.VMEM((slots, side, side), jnp.float32),
                pltpu.VMEM((slots, local * width // 128, 128), jnp.float32),
                pltpu.VMEM((slots, local * width // 128, 128), jnp.float32),
                pltpu.VMEM((PARTS, 16, 128 * slots), jnp.bfloat16),
                pltpu.VMEM((PARTS, slots, rows, width // PARTS), jnp.bfloat16),
                pltpu.VMEM((2, COLUMNS, ring, 16, 128 * slots), jnp.bfloat16),
                pltpu.VMEM((tile_count, 8, 384), jnp.float32),
                pltpu.VMEM((groups, per_group, 8, 384), jnp.float32),
                pltpu.VMEM((COLUMNS + ring, per_group, 8, 128), jnp.float32),
                pltpu.VMEM((COLUMNS + ring, per_group, 8, 128), jnp.float32),
                dma((7,)),
                dma((PARTS,)),
                dma((PARTS,)),
                dma((ring,)),
                dma((ring,)),
                dma((len(NEAR), 2)),
                dma((len(NEAR), 2)),
                dma((4, 4)),
                dma((4, 4)),
                dma((COLUMNS,)),
                dma((COLUMNS,)),
                dma((groups,)),
                dma((groups,)),
                dma((COLUMNS + ring,)),
                dma((COLUMNS + ring,)),
            ],
            compiler_params=pltpu.CompilerParams(
                collective_id=0, has_side_effects=True, vmem_limit_bytes=VMEM_BYTES
            ),
        )(
            *[
                pltpu.with_memory_space_constraint(x, pltpu.HBM)
                for x in (
                    layer_slot,
                    jnp.transpose(query_grads, (1, 0, 2)),
                    out_basis,
                    in_basis,
                    eigen_scale,
                    jnp.transpose(train_grads, (1, 0, 2)),
                )
            ]
        )

    return jax.shard_map(
        on_device,
        mesh=mesh,
        in_specs=(
            P("shard", "layer", None),
            P("layer", None, None),
            P("layer", None, None),
            P("layer", None, None),
            P("layer"),
            P("shard", "layer", None),
        ),
        out_specs=P("layer", "shard"),
        check_vma=False,
    )
```

time: 332 us -> 46.8 us (0.14); the launches traced: 325 us -> 46.6 us
  waiting for transfers between devices: 105 us -> 0 us
  local copies, waits for them, and re-layouts: 71.3 us -> 0.6 us
  matrix products: 65.7 us -> 0 us
  blocking collectives: 53.8 us -> 0 us
  Pallas kernels: 0 us -> 46 us
  other arithmetic: 14.8 us -> 0 us
  between operations: 14.7 us -> 0.01 us
    all_gather x1 -> x0, waiting for transfers between devices: 105 us -> none  [on_device(): gathered = lax.all_gather(query_grads, 'shard', axis=0, tiled=True)]
    dot_general x14 -> x0, matrix products: 65.7 us -> none  [the longest x3 25.3 us: precondition_layer(): back = jnp.einsum('ab,nbd->nad', left_basis, rotated, precision=high)]
    unnamed x1 -> x0, blocking collectives: 53.8 us -> none
    pallas_call x0 -> x1, Pallas kernels: none -> 46 us  [on_device(): pl.pallas_call(functools.partial(kernel, ring, groups), out_shape=jax.Sha...]
    convert_element_type x3 -> x0, local copies, waits for them, and re-layouts: 16.9 us -> none  [precondition_all(): pieces.append(result.reshape(count, width).astype(jnp.bfloat16))]
    reshape x3 -> x0, local copies, waits for them, and re-layouts: 15.1 us -> none  [precondition_all(): queries[:, layer_index].astype(jnp.float32).reshape(count, side, side)]
    transpose x3 -> x0, local copies, waits for them, and re-layouts: 13.5 us -> none  [precondition_layer(): back = jnp.einsum('ab,nbd->nad', left_basis, rotated, precision=high)]
    unnamed x17 -> x1, local copies, waits for them, and re-layouts: 13.6 us -> 0.6 us
  transfers between devices with their start and end apart: 1 -> 0, of which waited for: 1 -> 0; matrix products, arithmetic and copies ran while one was open for 1% -> 0% of each run, Pallas kernels for 0% -> 0%
where the time goes in v4:
time: 46.8 us; the launch traced here: 46.6 us
  Pallas kernels  46 us (98%)
  local copies, waits for them, and re-layouts  0.6 us (1%)
    pallas_call x1, Pallas kernels, on_device(): pl.pallas_call(functools.partial(kernel, ring, groups), out_shape=jax.Sha...  46 us

profile of v4, /device:TPU:1, one launch (start us, length us, event | category | flops | bytes accessed | tf_op | source)
XLA Modules:
  0.0 46.6 jit_solution(6030031348529856840)
XLA Ops:
  0.0 46.0 %shard_map.64 = f32[8,32]{1,0:T(8,128)S(1)} custom-call(s32[3]{0:T(128)} %slot_hbm.1, bf16[3,4,4096]{2,1,0:T(4,128)(2,1)} %bitcast.3, f32[3,64,64]{2,1,0:T(8,128)} %s_hbm.1, f32[3,64,64]{2,1,0:T(8,128)} %a_hbm.1, f32[3,64,64]{2,1,0:T(8,128)} %e_hbm.1, bf16[3,32,4096]{2,1,0:T(8,128)(2,1)} %bitcast.2), custom_call_target="tpu_custom_call" | custom-call | tf_op jit(solution)/shard_map/pallas_call | solution.py:412
  46.1 0.6 %copy.8 = f32[8,32]{1,0:T(8,128)} copy(f32[8,32]{1,0:T(8,128)S(1)} %shard_map.64) | data formatting | bytes 2048

commit v5 on v4

--- a/solution.py
+++ b/solution.py
@@ -129,17 +129,6 @@
             src_ref=src, dst_ref=dst, send_sem=send, recv_sem=recv, device_id=(to_shard, to_group), device_id_type=MESH
         )
 
-    barrier = pltpu.get_barrier_semaphore()
-    partners = [(at(column, shifted(by)), group) for by in range(1, ring)]
-    partners += [(at(c, level), group) for c in columns[1:]]
-    for who in partners:
-        pl.semaphore_signal(barrier, inc=1, device_id=who, device_id_type=MESH)
-
-    def greet(d, carry):
-        pl.semaphore_signal(barrier, inc=1, device_id=(shard, lax.rem(group + d, groups)), device_id_type=MESH)
-        return carry
-
-    lax.fori_loop(1, groups, greet, 0)
     loads = []
     for i, (src, dst) in enumerate(
         [(q_hbm, q_ref), (a_hbm, a_ref), (s_hbm, s_ref), (e_hbm, e_ref), (slot_hbm, slot_ref)]
@@ -148,8 +137,18 @@
         copy.start()
         loads.append(copy)
 
-    pl.semaphore_wait(barrier, len(partners) + groups - 1)
-
+
+    barrier = pltpu.get_barrier_semaphore()
+    partners = [(at(column, shifted(by)), group) for by in range(1, ring)]
+    partners += [(at(c, level), group) for c in columns[1:]]
+    for who in partners:
+        pl.semaphore_signal(barrier, inc=1, device_id=who, device_id_type=MESH)
+
+    def greet(d, carry):
+        pl.semaphore_signal(barrier, inc=1, device_id=(shard, lax.rem(group + d, groups)), device_id_type=MESH)
+        return carry
+
+    lax.fori_loop(1, groups, greet, 0)
     span = train_ref.shape[2] // PARTS
 
     def part_of_train(part):
@@ -175,15 +174,11 @@
 
     @pl.when(core == 0)
     def _():
-        for who in (FIRST, SECOND):
-            train_to_column(who, 0).start()
         for half in range(2):
             keep_for_column(half).start()
 
     @pl.when(core == 1)
     def _():
-        for i in (2, 6):
-            train_to_level(i).start()
         keep_for_level().start()
 
     for copy in loads:
@@ -191,6 +186,8 @@
     for slot in range(slots):
         index = lax.rem(slot_ref[slot], slots)
         precondition_slot(index, slot, q_ref, s_ref, a_ref, e_ref, rows_ref, turned_ref, blocks_ref)
+
+    pl.semaphore_wait(barrier, len(partners) + groups - 1)
 
     @pl.when(core == 0)
     def _():
@@ -212,12 +209,14 @@
 
         for who in (FIRST, SECOND, ACROSS):
             own_to_column(who).start()
-        for who in (FIRST, SECOND):
-            train_to_column(who, 1).start()
         for half in range(2):
             gathered[half, OWN, level] = blocks_ref[2 * column + half]
         for i in range(len(NEAR)):
             near_copy(i, 0).start()
+        for who in (FIRST, SECOND):
+            train_to_column(who, 0).start()
+        for who in (FIRST, SECOND):
+            train_to_column(who, 1).start()
         for who in (FIRST, SECOND, ACROSS):
             own_to_column(who).wait_recv()
         for i in range(len(NEAR)):
@@ -275,7 +274,7 @@
         order = (4, 3, 5, 2, 6, 1, 7)
         for i in order:
             own_to_level(i).start()
-        for i in (1, 7, 3, 5, 4):
+        for i in (2, 6, 1, 7, 3, 5, 4):
             train_to_level(i).start()
         gathered[0, OWN, level] = blocks_ref[level]
         for i in order:
@@ -354,11 +353,8 @@
             tiles.at[pl.ds(to * per_group, per_group)], tiles_in.at[d], r_send.at[d], r_recv.at[d], shard, to
         )
 
-    def send_tile(d, carry):
+    for d in sorted(range(1, groups), key=lambda d: abs(2 * d - groups)):
         group_copy(d).start()
-        return carry
-
-    lax.fori_loop(1, groups, send_tile, 0)
     sums = [tiles[pl.ds(group * per_group, per_group)], None]
     for d in range(1, groups):
         group_copy(d).wait_recv()

time: 46.8 us -> 45.4 us (0.970)
  Pallas kernels: 46 us -> 44.6 us
    pallas_call x1, Pallas kernels: 46 us -> 44.6 us  [on_device(): pl.pallas_call(functools.partial(kernel, ring, groups), out_shape=jax.Sha...]
where the time goes in v5:
time: 45.4 us; the launch traced here: 45.2 us
  Pallas kernels  44.6 us (98%)
  local copies, waits for them, and re-layouts  0.6 us (1%)
    pallas_call x1, Pallas kernels, on_device(): pl.pallas_call(functools.partial(kernel, ring, groups), out_shape=jax.Sha...  44.6 us

profile of v5, /device:TPU:1, one launch (start us, length us, event | category | flops | bytes accessed | tf_op | source)
XLA Modules:
  0.0 45.2 jit_solution(7975798323977698205)
XLA Ops:
  0.0 44.6 %shard_map.64 = f32[8,32]{1,0:T(8,128)S(1)} custom-call(s32[3]{0:T(128)} %slot_hbm.1, bf16[3,4,4096]{2,1,0:T(4,128)(2,1)} %bitcast.3, f32[3,64,64]{2,1,0:T(8,128)} %s_hbm.1, f32[3,64,64]{2,1,0:T(8,128)} %a_hbm.1, f32[3,64,64]{2,1,0:T(8,128)} %e_hbm.1, bf16[3,32,4096]{2,1,0:T(8,128)(2,1)} %bitcast.2), custom_call_target="tpu_custom_call" | custom-call | tf_op jit(solution)/shard_map/pallas_call | solution.py:408
  44.6 0.6 %copy.8 = f32[8,32]{1,0:T(8,128)} copy(f32[8,32]{1,0:T(8,128)S(1)} %shard_map.64) | data formatting | bytes 2048

commit v6 on v5

--- a/solution.py
+++ b/solution.py
@@ -14,7 +14,7 @@
 COLUMNS = 4
 OWN, FIRST, SECOND, ACROSS = range(4)
 NEAR = (2, -2, 1, -1)
-LOTS = (slice(0, 1), slice(1, 4), slice(0, 2), slice(2, 4))
+LOTS = (slice(0, 1), slice(1, 3), slice(3, 4), slice(0, 2), slice(2, 4))
 VMEM_BYTES = 40 * 1024 * 1024
 
 
@@ -85,6 +85,7 @@
     blocks_ref,
     train_part,
     gathered,
+    scored,
     tiles,
     tiles_in,
     pair_out,
@@ -189,89 +190,137 @@
 
     pl.semaphore_wait(barrier, len(partners) + groups - 1)
 
+    def score(whos, levels):
+        many = whos.stop - whos.start
+        count = many * len(levels)
+
+        def blocks_of(part):
+            value = [gathered[part, whos, pl.ds(lev, 1)].reshape(16 * many, 128 * slots) for lev in levels]
+            return jnp.concatenate(value, axis=0) if len(value) > 1 else value[0]
+
+        left = [blocks_of(part) for part in (0, 1 - core)]
+        squares = [value.astype(jnp.float32) for value in left]
+        squares = squares[0] * squares[0] + jnp.where(core == 0, squares[1] * squares[1], 0.0)
+        norm = squares[:, :128]
+        for slot in range(1, slots):
+            norm = norm + squares[:, 128 * slot : 128 * (slot + 1)]
+        lane = lax.broadcasted_iota(jnp.int32, (count, 8, 128), 2) // 32
+        same = lax.broadcasted_iota(jnp.int32, (count, 16, 128), 1) // 4 == (
+            lax.broadcasted_iota(jnp.int32, (count, 16, 128), 2) // 32
+        )
+
+        def queries_of(value):
+            value = value[:, :8] + value[:, 8:]
+            return value + pltpu.roll(value, 4, 1)
+
+        low = jnp.zeros((count, 8, 128), jnp.float32)
+        high = low
+        for i in range(PARTS):
+            right = jnp.concatenate(
+                [
+                    jnp.concatenate(
+                        [train_part[i, slot, :, 128 * sub : 128 * (sub + 1)] for slot in range(slots)], axis=1
+                    )
+                    for sub in range(4)
+                ],
+                axis=0,
+            )
+            product = lax.dot_general(
+                left[i % 2], right, (((1,), (1,)), ((), ())), preferred_element_type=jnp.float32
+            ).reshape(count, 16, 128)
+            value = queries_of(jnp.where(same, product, 0.0))
+            value = value + pltpu.roll(value, 64, 2)
+            value = value + pltpu.roll(value, 32, 2)
+            low = low + jnp.where(lane == jnp.where(core == 0, i // 2, i), value, 0.0)
+            if i >= 4:
+                high = high + jnp.where(lane == i - 4, value, 0.0)
+        norm = queries_of(norm.reshape(count, 16, 128))
+        norm = jnp.broadcast_to(jnp.sum(norm, axis=2, keepdims=True), (count, 8, 128))
+        for k, value in enumerate((low, high, norm)):
+            for place, lev in enumerate(levels):
+                scored[k, whos, pl.ds(lev, 1)] = value[many * place : many * (place + 1)].reshape(many, 1, 8, 128)
+
+    def own_to_column(who):
+        return remote(
+            blocks_ref.at[pl.ds(2 * columns[who], 2)],
+            gathered.at[:, who, level],
+            q_send.at[who],
+            q_recv.at[who],
+            at(columns[who], level),
+        )
+
+    def block_of(lot, by):
+        return gathered.at[:, LOTS[lot], shifted(by)]
+
+    def near_copy(i, lot, source=0):
+        block = block_of(lot, source)
+        return remote(block, block, near_send.at[i, lot], near_recv.at[i, lot], at(column, shifted(NEAR[i])))
+
+    def far_copy(row, lot, source, on):
+        block = block_of(lot, source)
+        return remote(block, block, far_send.at[row, lot], far_recv.at[row, lot], at(column, shifted(on)))
+
+    far = [(row, lot, (-2, 2)[row], (1, -1)[row]) for lot in range(3) for row in range(2)]
+    far += [(0, 3, -2, 2), (1, 4, 2, -2)]
+
+    def own_to_level(i):
+        to = shifted(-i)
+        return remote(
+            blocks_ref.at[to], gathered.at[0, OWN, level], q_send.at[i], q_recv.at[i], at(column, to)
+        )
+
+    def levels_to_column(who):
+        return remote(
+            gathered.at[0, OWN],
+            gathered.at[0, who],
+            across_send.at[who],
+            across_recv.at[who],
+            at(columns[who], level),
+        )
+
+    order = (4, 3, 5, 2, 6, 1, 7)
+
     @pl.when(core == 0)
     def _():
-        def own_to_column(who):
-            return remote(
-                blocks_ref.at[pl.ds(2 * columns[who], 2)],
-                gathered.at[:, who, level],
-                q_send.at[who],
-                q_recv.at[who],
-                at(columns[who], level),
-            )
-
-        def block_of(lot, by):
-            return gathered.at[:, LOTS[lot], shifted(by)]
-
-        def near_copy(i, lot, source=0):
-            block = block_of(lot, source)
-            return remote(block, block, near_send.at[i, lot], near_recv.at[i, lot], at(column, shifted(NEAR[i])))
-
         for who in (FIRST, SECOND, ACROSS):
             own_to_column(who).start()
         for half in range(2):
             gathered[half, OWN, level] = blocks_ref[2 * column + half]
         for i in range(len(NEAR)):
             near_copy(i, 0).start()
+        for half in range(2):
+            train_to_column(ACROSS, half).start()
         for who in (FIRST, SECOND):
             train_to_column(who, 0).start()
         for who in (FIRST, SECOND):
             train_to_column(who, 1).start()
-        for who in (FIRST, SECOND, ACROSS):
+        for who in (FIRST, SECOND):
             own_to_column(who).wait_recv()
         for i in range(len(NEAR)):
             near_copy(i, 1).start()
-        for half in range(2):
-            train_to_column(ACROSS, half).start()
-
-        def far_copy(row, lot, source, on):
-            block = block_of(lot, source)
-            return remote(block, block, far_send.at[row, lot], far_recv.at[row, lot], at(column, shifted(on)))
-
-        far = [(0, 0, -2, 1), (1, 0, 2, -1), (0, 1, -2, 1), (1, 1, 2, -1), (2, 2, -2, 2), (3, 3, 2, -2)]
-        for lot in range(2):
+        own_to_column(ACROSS).wait_recv()
+        for i in range(len(NEAR)):
+            near_copy(i, 2).start()
+        for lot in range(3):
             for i in range(2):
                 near_copy(i, lot, -NEAR[i]).wait_recv()
-        for row, lot, source, on in far:
-            far_copy(row, lot, source, on).start()
-        for lot in range(2):
+            for row, which, source, on in far:
+                if which == lot or lot == 2 and which > 2:
+                    far_copy(row, which, source, on).start()
+        for lot in range(3):
             for i in range(2, len(NEAR)):
                 near_copy(i, lot, -NEAR[i]).wait_recv()
-        for row, lot, source, on in far:
-            far_copy(row, lot, source - on, on).wait_recv()
         for half in range(2):
             keep_for_column(half).wait()
             for who in (FIRST, SECOND, ACROSS):
                 train_to_column(who, half).wait_recv()
-        for half in range(2):
-            for who in (FIRST, SECOND, ACROSS):
-                train_to_column(who, half).wait_send()
-        for who in (FIRST, SECOND, ACROSS):
-            own_to_column(who).wait_send()
-        for lot in range(2):
-            for i in range(len(NEAR)):
-                near_copy(i, lot).wait_send()
+        score(slice(0, COLUMNS), [level] + [shifted(by) for by in NEAR])
         for row, lot, source, on in far:
-            far_copy(row, lot, source, on).wait_send()
+            far_copy(row, lot, source - on, on).wait_recv()
+        score(slice(0, COLUMNS), [shifted(by) for by in (3, 4, 5)])
 
     @pl.when(core == 1)
     def _():
-        def own_to_level(i):
-            to = shifted(-i)
-            return remote(
-                blocks_ref.at[to], gathered.at[0, OWN, level], q_send.at[i], q_recv.at[i], at(column, to)
-            )
-
-        def levels_to_column(who):
-            return remote(
-                gathered.at[0, OWN],
-                gathered.at[0, who],
-                across_send.at[who],
-                across_recv.at[who],
-                at(columns[who], level),
-            )
-
-        order = (4, 3, 5, 2, 6, 1, 7)
         for i in order:
             own_to_level(i).start()
         for i in (2, 6, 1, 7, 3, 5, 4):
@@ -285,65 +334,23 @@
                 q_recv.at[i],
                 at(column, shifted(-i)),
             ).wait_recv()
-        for who in (ACROSS, FIRST, SECOND):
+        for who in (FIRST, SECOND, ACROSS):
             levels_to_column(who).start()
-        for who in (ACROSS, FIRST, SECOND):
-            levels_to_column(who).wait_recv()
         keep_for_level().wait()
         for i in range(1, ring):
             train_to_level(i).wait_recv()
-        for i in range(1, ring):
-            train_to_level(i).wait_send()
-            own_to_level(i).wait_send()
+        score(slice(0, 1), list(range(ring)))
         for who in (ACROSS, FIRST, SECOND):
-            levels_to_column(who).wait_send()
-
-    count = COLUMNS * ring
-    left = [gathered[part].reshape(16 * count, 128 * slots) for part in (0, 1 - core)]
-    squares = [value.astype(jnp.float32) for value in left]
-    squares = squares[0] * squares[0] + jnp.where(core == 0, squares[1] * squares[1], 0.0)
-    norm = squares[:, :128]
-    for slot in range(1, slots):
-        norm = norm + squares[:, 128 * slot : 128 * (slot + 1)]
-
-    row = lax.broadcasted_iota(jnp.int32, (tile_count, 8, 128), 1)
-    lane = lax.broadcasted_iota(jnp.int32, (tile_count, 8, 128), 2) // 32
-    same = lax.broadcasted_iota(jnp.int32, (count, 16, 128), 1) // 4 == (
-        lax.broadcasted_iota(jnp.int32, (count, 16, 128), 2) // 32
-    )
-
-    def queries_of(value):
-        value = value[:, :8] + value[:, 8:]
-        value = (value + pltpu.roll(value, 4, 1)).reshape(tile_count, 2, 8, 128)
-        return jnp.where(row < 4, value[:, 0], value[:, 1])
-
-    low = jnp.zeros((tile_count, 8, 128), jnp.float32)
-    high = low
-    for i in range(PARTS):
-        right = jnp.concatenate(
-            [
-                jnp.concatenate([train_part[i, slot, :, 128 * sub : 128 * (sub + 1)] for slot in range(slots)], axis=1)
-                for sub in range(4)
-            ],
-            axis=0,
-        )
-        product = lax.dot_general(
-            left[i % 2], right, (((1,), (1,)), ((), ())), preferred_element_type=jnp.float32
-        ).reshape(count, 16, 128)
-        value = queries_of(jnp.where(same, product, 0.0))
-        value = value + pltpu.roll(value, 64, 2)
-        value = value + pltpu.roll(value, 32, 2)
-        low = low + jnp.where(lane == jnp.where(core == 0, i // 2, i), value, 0.0)
-        if i >= 4:
-            high = high + jnp.where(lane == i - 4, value, 0.0)
-    norm = jnp.sum(queries_of(norm.reshape(count, 16, 128)), axis=2, keepdims=True)
+            levels_to_column(who).wait_recv()
+        score(slice(1, COLUMNS), list(range(ring)))
+
+    row = lax.broadcasted_iota(jnp.int32, (ring // 2, 8, 128), 1)
     per_column = tile_count // COLUMNS
     for who in range(COLUMNS):
         place = pl.ds(columns[who] * per_column, per_column)
-        some = slice(who * per_column, (who + 1) * per_column)
-        tiles[place, :, :128] = low[some]
-        tiles[place, :, 128:256] = high[some]
-        tiles[place, :, 256:] = jnp.broadcast_to(norm[some], (per_column, 8, 128))
+        for k in range(3):
+            value = scored[k, who].reshape(ring // 2, 2, 8, 128)
+            tiles[place, :, 128 * k : 128 * (k + 1)] = jnp.where(row < 4, value[:, 0], value[:, 1])
 
     per_group = tile_count // groups
 
@@ -384,6 +391,27 @@
         pair_copy(j).wait_recv()
         answer = answer + pair_in[j]
     out_ref[...] = (answer[:, :, :32] / jnp.sqrt(answer[:, :, 32:33] + EPSILON)).reshape(out_ref.shape)
+
+    @pl.when(core == 0)
+    def _():
+        for half in range(2):
+            for who in (FIRST, SECOND, ACROSS):
+                train_to_column(who, half).wait_send()
+        for who in (FIRST, SECOND, ACROSS):
+            own_to_column(who).wait_send()
+        for lot in range(3):
+            for i in range(len(NEAR)):
+                near_copy(i, lot).wait_send()
+        for row, lot, source, on in far:
+            far_copy(row, lot, source, on).wait_send()
+
+    @pl.when(core == 1)
+    def _():
+        for i in range(1, ring):
+            train_to_level(i).wait_send()
+            own_to_level(i).wait_send()
+        for who in (ACROSS, FIRST, SECOND):
+            levels_to_column(who).wait_send()
 
     def tile_sent(d, carry):
         group_copy(d).wait_send()
@@ -421,6 +449,7 @@
                 pltpu.VMEM((PARTS, 16, 128 * slots), jnp.bfloat16),
                 pltpu.VMEM((PARTS, slots, rows, width // PARTS), jnp.bfloat16),
                 pltpu.VMEM((2, COLUMNS, ring, 16, 128 * slots), jnp.bfloat16),
+                pltpu.VMEM((3, COLUMNS, ring, 8, 128), jnp.float32),
                 pltpu.VMEM((tile_count, 8, 384), jnp.float32),
                 pltpu.VMEM((groups, per_group, 8, 384), jnp.float32),
                 pltpu.VMEM((COLUMNS + ring, per_group, 8, 128), jnp.float32),
@@ -430,10 +459,10 @@
                 dma((PARTS,)),
                 dma((ring,)),
                 dma((ring,)),
-                dma((len(NEAR), 2)),
-                dma((len(NEAR), 2)),
-                dma((4, 4)),
-                dma((4, 4)),
+                dma((len(NEAR), 3)),
+                dma((len(NEAR), 3)),
+                dma((2, 5)),
+                dma((2, 5)),
                 dma((COLUMNS,)),
                 dma((COLUMNS,)),
                 dma((groups,)),

time: 45.4 us -> 44.3 us (0.976)
  Pallas kernels: 44.6 us -> 43.5 us
    pallas_call x1, Pallas kernels: 44.6 us -> 43.5 us  [on_device(): pl.pallas_call(functools.partial(kernel, ring, groups), out_shape=jax.Sha...]
where the time goes in v6:
time: 44.3 us; the launch traced here: 44.1 us
  Pallas kernels  43.5 us (98%)
  local copies, waits for them, and re-layouts  0.6 us (1%)
    pallas_call x1, Pallas kernels, on_device(): pl.pallas_call(functools.partial(kernel, ring, groups), out_shape=jax.Sha...  43.5 us

profile of v6, /device:TPU:1, one launch (start us, length us, event | category | flops | bytes accessed | tf_op | source)
XLA Modules:
  0.0 44.1 jit_solution(6289670081416082069)
XLA Ops:
  0.0 43.5 %shard_map.64 = f32[8,32]{1,0:T(8,128)S(1)} custom-call(s32[3]{0:T(128)} %slot_hbm.1, bf16[3,4,4096]{2,1,0:T(4,128)(2,1)} %bitcast.3, f32[3,64,64]{2,1,0:T(8,128)} %s_hbm.1, f32[3,64,64]{2,1,0:T(8,128)} %a_hbm.1, f32[3,64,64]{2,1,0:T(8,128)} %e_hbm.1, bf16[3,32,4096]{2,1,0:T(8,128)(2,1)} %bitcast.2), custom_call_target="tpu_custom_call" | custom-call | tf_op jit(solution)/shard_map/pallas_call | solution.py:436
  43.5 0.6 %copy.8 = f32[8,32]{1,0:T(8,128)} copy(f32[8,32]{1,0:T(8,128)S(1)} %shard_map.64) | data formatting | bytes 2048

commit v7 on v6

--- a/solution.py
+++ b/solution.py
@@ -88,6 +88,7 @@
     scored,
     tiles,
     tiles_in,
+    summed,
     pair_out,
     pair_in,
     local_sem,
@@ -362,32 +363,52 @@
 
     for d in sorted(range(1, groups), key=lambda d: abs(2 * d - groups)):
         group_copy(d).start()
-    sums = [tiles[pl.ds(group * per_group, per_group)], None]
-    for d in range(1, groups):
-        group_copy(d).wait_recv()
-        sums[d % 2] = tiles_in[d] if sums[d % 2] is None else sums[d % 2] + tiles_in[d]
-    by_column = jnp.where(core == 0, sums[0], sums[1])
-    by_level = jnp.where(core == 0, sums[1], sums[0])
-
-    scores_of = [by_column[:, :, :128]] * COLUMNS + [by_level[:, :, :128]] * 4 + [by_level[:, :, 128:256]] * 4
-    squares_of = [by_column[:, :, 256:]] * COLUMNS + [by_level[:, :, 256:]] * ring
+
+    def sum_of(which):
+        def add(even):
+            value = tiles[pl.ds(group * per_group, per_group)] if even else None
+            for d in range(2 if even else 1, groups, 2):
+                group_copy(d).wait_recv()
+                value = tiles_in[d] if value is None else value + tiles_in[d]
+            summed[which] = value
+
+        @pl.when(core == which)
+        def _():
+            add(True)
+
+        @pl.when(core != which)
+        def _():
+            add(False)
+
     is_score = lax.broadcasted_iota(jnp.int32, (per_group, 8, 128), 2) < 32
 
     def packed(j):
-        turned = scores_of[j] if j % 4 == 0 else pltpu.roll(scores_of[j], 128 - 32 * (j % 4), 2)
-        return jnp.where(is_score, turned, squares_of[j])
+        which = 0 if j < COLUMNS else 1
+        start = 128 if j >= COLUMNS + 4 else 0
+        scores = summed[which, :, :, start : start + 128]
+        turned = scores if j % 4 == 0 else pltpu.roll(scores, 128 - 32 * (j % 4), 2)
+        return jnp.where(is_score, turned, summed[which, :, :, 256:])
 
     def pair_copy(j):
         to = at(columns[j], level) if j < COLUMNS else at(column, shifted(j - COLUMNS))
         return remote(pair_out.at[j], pair_in.at[j], p_send.at[j], p_recv.at[j], to)
 
-    others = [COLUMNS + i for i in (4, 3, 5)] + [ACROSS] + [COLUMNS + i for i in (2, 6)] + [FIRST, SECOND]
-    others += [COLUMNS + i for i in (1, 7)]
-    for j in others:
+    from_levels = [COLUMNS + i for i in (4, 3, 5, 2, 6, 1, 7)]
+    from_columns = [ACROSS, FIRST, SECOND]
+    others = from_levels + from_columns
+    sum_of(1)
+    for j in from_levels:
+        pair_out[j] = packed(j)
+        pair_copy(j).start()
+    sum_of(0)
+    for j in from_columns:
         pair_out[j] = packed(j)
         pair_copy(j).start()
     answer = packed(OWN) + packed(COLUMNS)
-    for j in reversed(others):
+    for j in reversed(from_levels):
+        pair_copy(j).wait_recv()
+        answer = answer + pair_in[j]
+    for j in reversed(from_columns):
         pair_copy(j).wait_recv()
         answer = answer + pair_in[j]
     out_ref[...] = (answer[:, :, :32] / jnp.sqrt(answer[:, :, 32:33] + EPSILON)).reshape(out_ref.shape)
@@ -452,6 +473,7 @@
                 pltpu.VMEM((3, COLUMNS, ring, 8, 128), jnp.float32),
                 pltpu.VMEM((tile_count, 8, 384), jnp.float32),
                 pltpu.VMEM((groups, per_group, 8, 384), jnp.float32),
+                pltpu.VMEM((2, per_group, 8, 384), jnp.float32),
                 pltpu.VMEM((COLUMNS + ring, per_group, 8, 128), jnp.float32),
                 pltpu.VMEM((COLUMNS + ring, per_group, 8, 128), jnp.float32),
                 dma((7,)),

time: 44.3 us -> 43.9 us (level)
  no operation moved by 1% of the time
where the time goes in v7:
time: 43.9 us; the launch traced here: 43.8 us
  Pallas kernels  43.1 us (98%)
  local copies, waits for them, and re-layouts  0.6 us (1%)
    pallas_call x1, Pallas kernels, on_device(): pl.pallas_call(functools.partial(kernel, ring, groups), out_shape=jax.Sha...  43.1 us

profile of v7, /device:TPU:1, one launch (start us, length us, event | category | flops | bytes accessed | tf_op | source)
XLA Modules:
  0.0 43.8 jit_solution(8162185210031906058)
XLA Ops:
  0.0 43.1 %shard_map.64 = f32[8,32]{1,0:T(8,128)S(1)} custom-call(s32[3]{0:T(128)} %slot_hbm.1, bf16[3,4,4096]{2,1,0:T(4,128)(2,1)} %bitcast.3, f32[3,64,64]{2,1,0:T(8,128)} %s_hbm.1, f32[3,64,64]{2,1,0:T(8,128)} %a_hbm.1, f32[3,64,64]{2,1,0:T(8,128)} %e_hbm.1, bf16[3,32,4096]{2,1,0:T(8,128)(2,1)} %bitcast.2), custom_call_target="tpu_custom_call" | custom-call | tf_op jit(solution)/shard_map/pallas_call | solution.py:457
  43.2 0.6 %copy.8 = f32[8,32]{1,0:T(8,128)} copy(f32[8,32]{1,0:T(8,128)S(1)} %shard_map.64) | data formatting | bytes 2048

commit v8 on v7

--- a/solution.py
+++ b/solution.py
@@ -290,11 +290,8 @@
         for i in range(len(NEAR)):
             near_copy(i, 0).start()
         for half in range(2):
-            train_to_column(ACROSS, half).start()
-        for who in (FIRST, SECOND):
-            train_to_column(who, 0).start()
-        for who in (FIRST, SECOND):
-            train_to_column(who, 1).start()
+            for who in (ACROSS, FIRST, SECOND):
+                train_to_column(who, half).start()
         for who in (FIRST, SECOND):
             own_to_column(who).wait_recv()
         for i in range(len(NEAR)):

time: 43.9 us -> 43.9 us (level)
  no operation moved by 1% of the time
where the time goes in v8:
time: 43.9 us; the launch traced here: 43.7 us
  Pallas kernels  43.1 us (98%)
  local copies, waits for them, and re-layouts  0.6 us (1%)
    pallas_call x1, Pallas kernels, on_device(): pl.pallas_call(functools.partial(kernel, ring, groups), out_shape=jax.Sha...  43.1 us

profile of v8, /device:TPU:1, one launch (start us, length us, event | category | flops | bytes accessed | tf_op | source)
XLA Modules:
  0.0 43.7 jit_solution(15457081622058661101)
XLA Ops:
  0.0 43.1 %shard_map.64 = f32[8,32]{1,0:T(8,128)S(1)} custom-call(s32[3]{0:T(128)} %slot_hbm.1, bf16[3,4,4096]{2,1,0:T(4,128)(2,1)} %bitcast.3, f32[3,64,64]{2,1,0:T(8,128)} %s_hbm.1, f32[3,64,64]{2,1,0:T(8,128)} %a_hbm.1, f32[3,64,64]{2,1,0:T(8,128)} %e_hbm.1, bf16[3,32,4096]{2,1,0:T(8,128)(2,1)} %bitcast.2), custom_call_target="tpu_custom_call" | custom-call | tf_op jit(solution)/shard_map/pallas_call | solution.py:454
  43.1 0.6 %copy.8 = f32[8,32]{1,0:T(8,128)} copy(f32[8,32]{1,0:T(8,128)S(1)} %shard_map.64) | data formatting | bytes 2048

commit v9 on v8

--- a/solution.py
+++ b/solution.py
@@ -321,7 +321,7 @@
     def _():
         for i in order:
             own_to_level(i).start()
-        for i in (2, 6, 1, 7, 3, 5, 4):
+        for i in (1, 7, 2, 6, 3, 5, 4):
             train_to_level(i).start()
         gathered[0, OWN, level] = blocks_ref[level]
         for i in order:

time: 43.9 us -> 44 us (level)
  no operation moved by 1% of the time
where the time goes in v9:
time: 44 us; the launch traced here: 43.9 us
  Pallas kernels  43.2 us (98%)
  local copies, waits for them, and re-layouts  0.6 us (1%)
    pallas_call x1, Pallas kernels, on_device(): pl.pallas_call(functools.partial(kernel, ring, groups), out_shape=jax.Sha...  43.2 us

profile of v9, /device:TPU:1, one launch (start us, length us, event | category | flops | bytes accessed | tf_op | source)
XLA Modules:
  0.0 43.9 jit_solution(15266932074218274585)
XLA Ops:
  0.0 43.2 %shard_map.64 = f32[8,32]{1,0:T(8,128)S(1)} custom-call(s32[3]{0:T(128)} %slot_hbm.1, bf16[3,4,4096]{2,1,0:T(4,128)(2,1)} %bitcast.3, f32[3,64,64]{2,1,0:T(8,128)} %s_hbm.1, f32[3,64,64]{2,1,0:T(8,128)} %a_hbm.1, f32[3,64,64]{2,1,0:T(8,128)} %e_hbm.1, bf16[3,32,4096]{2,1,0:T(8,128)(2,1)} %bitcast.2), custom_call_target="tpu_custom_call" | custom-call | tf_op jit(solution)/shard_map/pallas_call | solution.py:454
  43.3 0.6 %copy.8 = f32[8,32]{1,0:T(8,128)} copy(f32[8,32]{1,0:T(8,128)S(1)} %shard_map.64) | data formatting | bytes 2048
